TPU v7x, 32 devices: a whole 2x2x4 slice. The times are simulated.
32 devices in a mesh: occ: 2 (over core), row: 4 (over y, x), col: 4 (over z).
Axes of the slice: x: 2, y: 2, z: 4, core: 2. Of those that a mesh axis runs over, the one named last changes fastest.
Arguments:
- bra_factor: bfloat16 [3072, 2, 4096], P(('occ', 'col'), None, 'row'), may hold values from -0.5 to 0.5
- ket_factor: bfloat16 [3072, 2, 4096], P(('occ', 'row'), None, 'col'), may hold values from -0.5 to 0.5
- occ_energy: float32 [2], replicated, may hold values from -2 to -0.5
- virt_energy: float32 [4096], replicated, may hold values from 0.2 to 3
Outputs:
- amplitudes: bfloat16 [2, 2, 4096, 4096], P(None, None, 'row', 'col')
- gamma: float32 [3072, 2, 4096], P(('occ', 'col'), None, 'row')
All inputs are finite; a program needn't handle non-finite values.
Results may differ from a plain program's by a relative error of at most 0.002.
Values may be sent and summed in bfloat16 or wider, within the bound.
No kernel may reach another device: no remote copies, remote signals or barrier semaphores. Data moves between devices by JAX's collectives and lax.ppermute only.
A program may use at most 128 MiB of HBM per device.

v0:
```python
import jax
import jax.numpy as jnp
from jax import lax
from jax.sharding import PartitionSpec as P


def make_amplitudes(coulomb, occ_energy, virt_first, virt_second):
    denominator = (
        occ_energy[:, None, None, None]
        + occ_energy[None, :, None, None]
        - virt_first[None, None, :, None]
        - virt_second[None, None, None, :]
    )
    return ((2.0 * coulomb - jnp.transpose(coulomb, (1, 0, 2, 3))) / denominator).astype(
        jnp.bfloat16
    )


def on_device(bra_factor, ket_factor, occ_energy, virt_energy):
    a_width = bra_factor.shape[2]
    b_width = ket_factor.shape[2]
    ket_whole = lax.all_gather(ket_factor, "row", axis=0, tiled=True)
    row_index = lax.axis_index("row")
    col_index = lax.axis_index("col")
    virt_first = lax.dynamic_slice_in_dim(virt_energy, row_index * a_width, a_width, 0)
    virt_second = lax.dynamic_slice_in_dim(virt_energy, col_index * b_width, b_width, 0)
    partial_sum = jnp.einsum(
        "qia,qjb->ijab",
        lax.all_gather(bra_factor, "col", axis=0, tiled=True),
        ket_whole,
        preferred_element_type=jnp.float32,
    )
    batch_count = lax.axis_size("occ")
    pad_rows = (batch_count - a_width % batch_count) % batch_count
    padded = jnp.pad(partial_sum, ((0, 0), (0, 0), (0, pad_rows), (0, 0)))
    share_sum = lax.psum_scatter(padded, "occ", scatter_dimension=2, tiled=True)
    share_len = share_sum.shape[2]
    energy_padded = jnp.pad(virt_first, (0, pad_rows), constant_values=1.0)
    energy_share = lax.dynamic_slice_in_dim(
        energy_padded, lax.axis_index("occ") * share_len, share_len, 0
    )
    share_amps = make_amplitudes(share_sum, occ_energy, energy_share, virt_second)
    collected = lax.all_gather(share_amps, "occ", axis=2, tiled=True)
    amplitudes = collected[:, :, :a_width, :]
    gamma = lax.psum_scatter(
        jnp.einsum("ijab,qjb->qia", amplitudes, ket_whole, preferred_element_type=jnp.float32),
        "col",
        scatter_dimension=0,
        tiled=True,
    )
    return (amplitudes, gamma)


def solution(mesh):
    placed = (P(("occ", "col"), None, "row"), P(("occ", "row"), None, "col"), P(), P())
    return jax.shard_map(
        on_device,
        mesh=mesh,
        in_specs=placed,
        out_specs=(P(None, None, "row", "col"), P(("occ", "col"), None, "row")),
        check_vma=False,
    )
```

profile of v0, /device:TPU:0, one launch (start us, length us, event | category | flops | bytes accessed | tf_op | source)
XLA Modules:
  0.0 519.2 jit_solution(3891936038857893085)
XLA Ops:
  7.2 0.0 all-gather.6.cloned.1.call-start
  7.2 3.0 copy.7
  10.2 0.0 all-gather.6.cloned.1.call-update
  10.2 0.0 all-gather.4.cloned.1.call-start
  10.3 4.9 copy.6
  15.2 0.0 all-gather.4.cloned.1.call-update
  15.2 0.0 reduce-scatter.3.cloned.1.call-start
  15.3 113.2 %all-gather.6.cloned.1.call-done = bf16[1536,2,1024]{2,0,1:T(8,128)(2,1)} async-done(((bf16[384,2,1024]{2,0,1:T(8,128)(2,1)}), bf16[1536,2,1024]{2,0,1:T(8,128)(2,1)}) %all-gather.6.cloned.1.call-update) | async-done | bytes 6291472 | tf_op jit(solution)/shard_map/all_gather | solution.py:29
  128.4 70.6 %all-gather.4.cloned.1.call-done = bf16[1536,2,1024]{0,2,1:T(8,128)(2,1)} async-done(((bf16[384,2,1024]{0,2,1:T(8,128)(2,1)}), bf16[1536,2,1024]{0,2,1:T(8,128)(2,1)}) %all-gather.4.cloned.1.call-update) | async-done | bytes 6291472 | tf_op jit(solution)/shard_map/all_gather | solution.py:22
  199.1 19.4 %convolution_bitcast_fusion.1 = f32[2,2,1024,1024]{2,3,0,1:T(8,128)} fusion(bf16[1536,2,1024]{0,2,1:T(8,128)(2,1)} %all-gather.4.cloned.1.call-done, bf16[1536,2,1024]{2,0,1:T(8,128)(2,1)} %all-gather.6.cloned.1.call-done), kind=kOutput, calls=%fused_computation.5 | convolution fusion | flops 12884901888 | bytes 29360128 | tf_op jit(solution)/shard_map/qia,qjb->ijab/dot_general | solution.py:27
  218.5 0.0 copy-start
  218.5 0.0 reduce-scatter.3.cloned.1.call-update
  218.5 0.0 all-gather.8.cloned.1.call-start
  218.5 0.8 dynamic_slice.10
  219.3 0.7 dynamic_slice.11
  220.0 0.0 copy-done
  220.0 0.1 broadcast_add_fusion
  220.1 0.1 broadcast_subtract_fusion
  220.2 24.8 %reduce-scatter.3.cloned.1.call-done = f32[2,2,512,1024]{2,3,0,1:T(8,128)} async-done(((f32[2,2,1024,1024]{2,3,0,1:T(8,128)}), f32[2,2,512,1024]{2,3,0,1:T(8,128)}) %reduce-scatter.3.cloned.1.call-update) | async-done | bytes 8388624 | tf_op jit(solution)/shard_map/reduce_scatter | solution.py:36
  244.9 8.5 %fusion.1 = bf16[2,2,512,1024]{2,3,1,0:T(8,128)(2,1)} fusion(f32[2,2,512,1024]{2,3,0,1:T(8,128)} %reduce-scatter.3.cloned.1.call-done, f32[1024]{0:T(1024)S(1)} %dynamic_slice.11, f32[2,2,512]{2,1,0:T(2,128)S(1)} %broadcast_subtract_fusion), kind=kLoop, calls=%fused_computation.2 | loop fusion | flops 10485760 | bytes 12595200 | tf_op jit(solution)/shard_map/convert_element_type | solution.py:14
  253.4 0.0 all-gather.8.cloned.1.call-update
  253.5 0.0 reduce-scatter.5.cloned.1.call-start
  253.5 21.2 %all-gather.8.cloned.1.call-done = bf16[2,2,1024,1024]{2,3,1,0:T(8,128)(2,1)} async-done(((bf16[2,2,512,1024]{2,3,1,0:T(8,128)(2,1)}), bf16[2,2,1024,1024]{2,3,1,0:T(8,128)(2,1)}) %all-gather.8.cloned.1.call-update) | async-done | bytes 8388624 | tf_op jit(solution)/shard_map/all_gather | solution.py:43
  274.7 18.9 %convolution_bitcast_fusion = f32[1536,2,1024]{0,2,1:T(8,128)} fusion(bf16[2,2,1024,1024]{2,3,1,0:T(8,128)(2,1)} %all-gather.8.cloned.1.call-done, bf16[1536,2,1024]{0,2,1:T(8,128)(2,1)} %all-gather.4.cloned.1.call-done), kind=kOutput, calls=%fused_computation.4 | convolution fusion | flops 12884901888 | bytes 27262976 | tf_op jit(solution)/shard_map/ijab,qjb->qia/dot_general | solution.py:46
  293.7 0.0 reduce-scatter.5.cloned.1.call-update
  293.7 11.7 %copy.11 = bf16[2,2,1024,1024]{3,2,1,0:T(8,128)(2,1)} copy(bf16[2,2,1024,1024]{2,3,1,0:T(8,128)(2,1)} %all-gather.8.cloned.1.call-done) | data formatting | bytes 16777216
  305.4 201.5 %reduce-scatter.5.cloned.1.call-done = f32[384,2,1024]{0,2,1:T(8,128)} async-done(((f32[1536,2,1024]{0,2,1:T(8,128)}), f32[384,2,1024]{0,2,1:T(8,128)}) %reduce-scatter.5.cloned.1.call-update) | async-done | bytes 3145744 | tf_op jit(solution)/shard_map/reduce_scatter | solution.py:45
  506.9 5.8 %copy.12 = f32[384,2,1024]{2,1,0:T(2,128)} copy(f32[384,2,1024]{0,2,1:T(8,128)} %reduce-scatter.5.cloned.1.call-done) | data formatting | bytes 6291456
Async XLA Ops:
  7.2 121.3 %all-gather.6.cloned.1.call-start = ((), (), s32[]{:S(2)}) async-start(), calls=%async_computation.3 | async-start | bytes 7864320 | tf_op jit(solution)/shard_map/all_gather | solution.py:29
  10.2 188.8 %all-gather.4.cloned.1.call-start = ((), (), s32[]{:S(2)}) async-start(), calls=%async_computation.2 | async-start | bytes 7864320 | tf_op jit(solution)/shard_map/all_gather | solution.py:22
  15.2 229.7 %reduce-scatter.3.cloned.1.call-start = ((), (), s32[]{:S(2)}) async-start(), calls=%async_computation.4 | async-start | bytes 25165824 | tf_op jit(solution)/shard_map/reduce_scatter | solution.py:36
  218.5 1.6 copy-start
  218.5 56.2 %all-gather.8.cloned.1.call-start = ((), (), s32[]{:S(2)}) async-start(), calls=%async_computation.5 | async-start | bytes 12582912 | tf_op jit(solution)/shard_map/all_gather | solution.py:43
  253.5 253.4 %reduce-scatter.5.cloned.1.call-start = ((), (), s32[]{:S(2)}) async-start(), calls=%async_computation.6 | async-start | bytes 15728640 | tf_op jit(solution)/shard_map/reduce_scatter | solution.py:45
Sparse Core Ops, SparseCore 0:
  10.4 118.0 all-gather.5
  130.8 68.1 all-gather.3
  218.6 26.2 reduce-scatter.2
  253.6 21.0 all-gather.7
  293.8 213.0 reduce-scatter.4
where the time goes:
time: 520 us; the launch traced here: 519 us
  waiting for transfers between devices  431 us (83%)
  matrix products  38.3 us (7%)
  local copies, waits for them, and re-layouts  26.9 us (5%)
  between operations  13.8 us (3%)
  other arithmetic  8.66 us (2%)
    reduce_scatter x1, waiting for transfers between devices, on_device(): lax.psum_scatter(jnp.einsum('ijab,qjb->qia', amplitudes, ket_whole, prefe...  201 us
    all_gather x1, waiting for transfers between devices, on_device(): lax.all_gather(bra_factor, 'col', axis=0, tiled=True)  113 us
    all_gather x1, waiting for transfers between devices, on_device(): ket_whole = lax.all_gather(ket_factor, 'row', axis=0, tiled=True)  70.6 us
    unnamed x6, local copies, waits for them, and re-layouts  25.4 us
    reduce_scatter x1, waiting for transfers between devices, on_device(): share_sum = lax.psum_scatter(padded, 'occ', scatter_dimension=2, tiled=True)  24.8 us
    all_gather x1, waiting for transfers between devices, on_device(): collected = lax.all_gather(share_amps, 'occ', axis=2, tiled=True)  21.2 us
    dot_general x1, matrix products, on_device(): jnp.einsum('qia,qjb->ijab', lax.all_gather(bra_factor, 'col', axis=0, til...  19.4 us
    dot_general x1, matrix products, on_device(): jnp.einsum('ijab,qjb->qia', amplitudes, ket_whole, preferred_element_type...  18.9 us
  transfers between devices with their start and end apart: 5, of which 5 were waited for; matrix products, arithmetic and copies ran while one was open for 4% of the time, Pallas kernels for 0%

commit v1 on v0

--- a/solution.py
+++ b/solution.py
@@ -1,6 +1,10 @@
+import functools
+
 import jax
 import jax.numpy as jnp
 from jax import lax
+from jax.experimental import pallas as pl
+from jax.experimental.pallas import tpu as pltpu
 from jax.sharding import PartitionSpec as P
 
 
@@ -16,7 +20,7 @@
     )
 
 
-def on_device(bra_factor, ket_factor, occ_energy, virt_energy):
+def general(bra_factor, ket_factor, occ_energy, virt_energy):
     a_width = bra_factor.shape[2]
     b_width = ket_factor.shape[2]
     ket_whole = lax.all_gather(ket_factor, "row", axis=0, tiled=True)
@@ -51,7 +55,240 @@
     return (amplitudes, gamma)
 
 
+CHUNKS = 4
+
+
+def chunk_kernel(pieces, cols, groups, *refs):
+    count = 2 * len(pieces)
+    ket = refs[:count]
+    bra, occ_ref, first_ref, second_ref = refs[count : count + 4]
+    amps_ref, gamma_ref = refs[count + 4 : count + 6]
+    kv, bv, bt, t2, ket_sem, bra_sem = refs[count + 6 :]
+    width = first_ref.shape[0]
+    span = second_ref.shape[1]
+    part = span // groups
+    batch = bra.shape[2]
+    here_row, here_col = lax.axis_index("row"), lax.axis_index("col")
+
+    bra_copy = pltpu.make_async_copy(bra, bv, bra_sem)
+    bra_copy.start()
+    copies = []
+    for group in range(groups):
+        of_group = []
+        for q in range(2):
+            for index, (offset, begin, rows) in enumerate(pieces):
+                home = lax.bitwise_xor(here_row, offset)
+                to_row = pl.multiple_of(home * (2 * batch) + q * batch + begin, 16)
+                for j in range(2):
+                    columns = pl.ds(j * span + group * part, part)
+                    copy = pltpu.make_async_copy(
+                        ket[q * len(pieces) + index].at[:, columns],
+                        kv.at[pl.ds(to_row, rows), columns],
+                        ket_sem.at[group, q, index, j],
+                    )
+                    copy.start()
+                    of_group.append(copy)
+        copies.append(of_group)
+    bra_copy.wait()
+    for d in range(cols):
+        for q in range(2):
+            at = (2 * d + q) * batch
+            bt[:, at : at + batch] = bv[d, q].T
+    for group in range(groups):
+        for copy in copies[group]:
+            copy.wait()
+        tile = [
+            jnp.dot(
+                bt[...],
+                kv[:, j * span + group * part : j * span + (group + 1) * part],
+                preferred_element_type=jnp.float32,
+            )
+            for j in range(2)
+        ]
+        second = second_ref[:, group * part : (group + 1) * part]
+        for i in range(2):
+            for j in range(2):
+                direct = tile[j][i * width : (i + 1) * width, :]
+                exchange = tile[i][j * width : (j + 1) * width, :]
+                denominator = ((occ_ref[i] + occ_ref[j]) - first_ref[...]) - second
+                amps = ((2.0 * direct - exchange) / denominator).astype(jnp.bfloat16)
+                amps_ref[i, j, :, group * part : (group + 1) * part] = amps
+                t2[
+                    i * width : (i + 1) * width,
+                    j * span + group * part : j * span + (group + 1) * part,
+                ] = amps
+    for t in range(cols):
+        home = lax.rem(here_col + t, cols)
+        rows = pl.ds(pl.multiple_of(home * (2 * batch), 16), 2 * batch)
+        gamma_ref[t] = lax.dot_general(
+            kv[rows, :],
+            t2[...],
+            (((1,), (1,)), ((), ())),
+            preferred_element_type=jnp.float32,
+        )
+
+
+def run_chunk(ket, pieces, bra, occ_energy, first, second):
+    cols, _, batch, double = bra.shape
+    width = double // 2
+    span = second.shape[1]
+    groups = 4
+    total = cols * 2 * batch
+    flops = 2 * 2 * total * double * 2 * span
+    return pl.pallas_call(
+        functools.partial(chunk_kernel, pieces, cols, groups),
+        out_shape=(
+            jax.ShapeDtypeStruct((2, 2, width, span), jnp.bfloat16),
+            jax.ShapeDtypeStruct((cols, 2 * batch, double), jnp.float32),
+        ),
+        in_specs=[pl.BlockSpec(memory_space=pl.ANY)] * (len(ket) + 1)
+        + [
+            pl.BlockSpec(memory_space=pltpu.SMEM),
+            pl.BlockSpec(memory_space=pltpu.VMEM),
+            pl.BlockSpec(memory_space=pltpu.VMEM),
+        ],
+        out_specs=(
+            pl.BlockSpec(memory_space=pltpu.VMEM),
+            pl.BlockSpec(memory_space=pltpu.VMEM),
+        ),
+        scratch_shapes=[
+            pltpu.VMEM((total, 2 * span), jnp.bfloat16),
+            pltpu.VMEM(bra.shape, jnp.bfloat16),
+            pltpu.VMEM((double, total), jnp.bfloat16),
+            pltpu.VMEM((double, 2 * span), jnp.bfloat16),
+            pltpu.SemaphoreType.DMA((groups, 2, len(pieces), 2)),
+            pltpu.SemaphoreType.DMA,
+        ],
+        compiler_params=pltpu.CompilerParams(vmem_limit_bytes=48 * 2**20),
+        cost_estimate=pl.CostEstimate(
+            flops=flops, bytes_accessed=total * 2 * span * 2, transcendentals=0
+        ),
+    )(*ket, bra, occ_energy, first, second)
+
+
+def place_kernel(width, half, count, *refs):
+    own, other, out, sem = refs[:count], refs[count : 2 * count], refs[2 * count], refs[-1]
+    me = lax.axis_index("occ")
+    copies = []
+    for k in range(count):
+        for side, source in ((me, own[k]), (1 - me, other[k])):
+            at = pl.multiple_of(side * half + k * width, 16)
+            copy = pltpu.make_async_copy(
+                source, out.at[:, :, pl.ds(at, width), :], sem.at[len(copies)]
+            )
+            copy.start()
+            copies.append(copy)
+    for copy in copies:
+        copy.wait()
+
+
+def place(own, other):
+    count = len(own)
+    _, _, width, span = own[0].shape
+    return pl.pallas_call(
+        functools.partial(place_kernel, width, width * count, count),
+        out_shape=jax.ShapeDtypeStruct((2, 2, 2 * count * width, span), own[0].dtype),
+        in_specs=[pl.BlockSpec(memory_space=pl.ANY)] * (2 * count),
+        out_specs=pl.BlockSpec(memory_space=pl.ANY),
+        scratch_shapes=[pltpu.SemaphoreType.DMA((2 * count,))],
+        cost_estimate=pl.CostEstimate(
+            flops=0, bytes_accessed=16 * 2 * count * width * span, transcendentals=0
+        ),
+    )(*own, *other)
+
+
+def swap(x):
+    return lax.ppermute(x, "occ", [(0, 1), (1, 0)])
+
+
+def planar(x, offset):
+    return lax.ppermute(x, "row", [(r, r ^ offset) for r in range(4)])
+
+
+def sum_along(share, cols):
+    up = down = None
+    for step in range(cols - 1):
+        send_up = share[cols - 1 - step]
+        send_down = share[step + 1]
+        if step:
+            send_up, send_down = send_up + up, send_down + down
+        up = lax.ppermute(
+            send_up.astype(jnp.bfloat16), "col", [(c, c + 1) for c in range(step + 1)]
+        ).astype(jnp.float32)
+        down = lax.ppermute(
+            send_down.astype(jnp.bfloat16),
+            "col",
+            [(cols - 1 - c, cols - 2 - c) for c in range(step + 1)],
+        ).astype(jnp.float32)
+    return share[0] + up + down
+
+
+def planned(bra_factor, ket_factor, occ_energy, virt_energy):
+    batch, _, a_width = bra_factor.shape
+    b_width = ket_factor.shape[2]
+    half = a_width // 2
+    width = half // CHUNKS
+    cols = lax.axis_size("col")
+    me, row_index, col_index = (lax.axis_index(name) for name in ("occ", "row", "col"))
+
+    def rows_of(side):
+        part = lax.dynamic_slice_in_dim(bra_factor, side * half, half, 2)
+        part = part.reshape(batch, 2, CHUNKS, width).transpose(2, 0, 1, 3)
+        return part.reshape(CHUNKS, batch, 2 * width)
+
+    ket_own = ket_factor.reshape(batch, 2 * b_width)
+    ket_x = planar(ket_own, 1)
+    ket_y = planar(ket_own, 2)
+    cut = batch // 2
+    ket_far_y = planar(ket_x[:cut], 2)
+    ket_far_x = planar(ket_y[cut:], 1)
+    mine = [ket_own, ket_x, ket_y, ket_far_y, ket_far_x]
+    pieces = ((0, 0, batch), (1, 0, batch), (2, 0, batch), (3, 0, cut), (3, cut, batch - cut))
+    ket = mine + [swap(piece) for piece in mine]
+
+    bra_own = rows_of(me)
+    bra_other = swap(rows_of(1 - me))
+    second = lax.dynamic_slice_in_dim(virt_energy, col_index * b_width, b_width, 0)[None, :]
+    first_start = row_index * a_width + me * half
+
+    amps, sums = [], []
+    for k in range(CHUNKS):
+        bra = lax.all_gather(jnp.stack([bra_own[k], bra_other[k]]), "col", axis=0)
+        first = lax.dynamic_slice_in_dim(virt_energy, first_start + k * width, width, 0)
+        part, share = run_chunk(ket, pieces, bra, occ_energy, first[:, None], second)
+        amps.append(part)
+        sums.append(sum_along(share, cols))
+    amplitudes = place(amps, [swap(part) for part in amps])
+
+    def gathered(parts):
+        whole = jnp.stack(parts).reshape(CHUNKS, batch, 2, width)
+        return whole.transpose(1, 2, 0, 3).reshape(batch, 2, half)
+
+    kept = gathered([total[:batch] for total in sums])
+    received = gathered([swap(total[batch:]) for total in sums])
+    gamma = jnp.where(
+        me == 0,
+        jnp.concatenate([kept, received], axis=2),
+        jnp.concatenate([received, kept], axis=2),
+    )
+    return (amplitudes, gamma)
+
+
 def solution(mesh):
+    sizes = mesh.shape
+
+    def on_device(bra_factor, ket_factor, occ_energy, virt_energy):
+        fits = (
+            sizes["occ"] == 2
+            and sizes["row"] == 4
+            and sizes["col"] > 1
+            and bra_factor.shape[2] % (256 * CHUNKS) == 0
+            and ket_factor.shape[2] % 512 == 0
+            and bra_factor.shape[0] % 128 == 0
+        )
+        body = planned if fits else general
+        return body(bra_factor, ket_factor, occ_energy, virt_energy)
+
     placed = (P(("occ", "col"), None, "row"), P(("occ", "row"), None, "col"), P(), P())
     return jax.shard_map(
         on_device,

time: 520 us -> 597 us (1.15); the launches traced: 519 us -> 588 us
  waiting for transfers between devices: 431 us -> 124 us
  Pallas kernels: 0 us -> 305 us
  starting transfers between devices: 0.21 us -> 94 us
  matrix products: 38.3 us -> 0 us
  local copies, waits for them, and re-layouts: 26.9 us -> 38.9 us
    pallas_call x0 -> x5, Pallas kernels: none -> 305 us  [the longest x1 255 us: place(): pl.pallas_call(functools.partial(place_kernel, width, width * count, coun...]
    reduce_scatter x2 -> x0, waiting for transfers between devices: 226 us -> none  [the longest x1 201 us: on_device(): lax.psum_scatter(jnp.einsum('ijab,qjb->qia', amplitudes, ket_whole, prefe...]
    all_gather x3 -> x4, waiting for transfers between devices: 205 us -> 43.1 us  [planned(): bra = lax.all_gather(jnp.stack([bra_own[k], bra_other[k]]), 'col', axis=0)]
    ppermute x0 -> x42, starting transfers between devices: none -> 93.9 us  [the longest x12 72.6 us: sum_along(): lax.ppermute(send_up.astype(jnp.bfloat16), 'col', [(c, c + 1) for c in ra...]
    ppermute x0 -> x42, waiting for transfers between devices: none -> 80.9 us  [the longest x4 48.7 us: planar(): return lax.ppermute(x, 'row', [(r, r ^ offset) for r in range(4)])]
    dot_general x2 -> x0, matrix products: 38.3 us -> none  [the longest x1 19.4 us: on_device(): jnp.einsum('qia,qjb->ijab', lax.all_gather(bra_factor, 'col', axis=0, til...]
    unnamed x6 -> x43, local copies, waits for them, and re-layouts: 25.4 us -> 11.1 us
    convert_element_type x0 -> x4, local copies, waits for them, and re-layouts: none -> 9.3 us  [sum_along(): send_up.astype(jnp.bfloat16)]
  transfers between devices with their start and end apart: 5 -> 46, of which waited for: 5 -> 14; matrix products, arithmetic and copies ran while one was open for 4% -> 5% of each run, Pallas kernels for 0% -> 52%
where the time goes in v1:
time: 597 us; the launch traced here: 588 us
  Pallas kernels  305 us (51%)
  waiting for transfers between devices  124 us (21%)
  starting transfers between devices  94 us (16%)
  local copies, waits for them, and re-layouts  38.9 us (7%)
  between operations  15.1 us (3%)
  other arithmetic  10.5 us (2%)
    pallas_call x1, Pallas kernels, place(): pl.pallas_call(functools.partial(place_kernel, width, width * count, coun...  255 us
    ppermute x12, starting transfers between devices, sum_along(): lax.ppermute(send_up.astype(jnp.bfloat16), 'col', [(c, c + 1) for c in ra...  72.6 us
    pallas_call x4, Pallas kernels, run_chunk(): pl.pallas_call(functools.partial(chunk_kernel, pieces, cols, groups), out...  50.1 us
    ppermute x4, waiting for transfers between devices, planar(): return lax.ppermute(x, 'row', [(r, r ^ offset) for r in range(4)])  48.7 us
    all_gather x4, waiting for transfers between devices, planned(): bra = lax.all_gather(jnp.stack([bra_own[k], bra_other[k]]), 'col', axis=0)  43.1 us
    ppermute x12, waiting for transfers between devices, sum_along(): lax.ppermute(send_up.astype(jnp.bfloat16), 'col', [(c, c + 1) for c in ra...  24.4 us
  transfers between devices with their start and end apart: 46, of which 14 were waited for; matrix products, arithmetic and copies ran while one was open for 5% of the time, Pallas kernels for 52%

profile of v1, /device:TPU:0, one launch (start us, length us, event | category | flops | bytes accessed | tf_op | source)
XLA Modules:
  0.0 587.9 jit_solution(14186809405052664340)
XLA Ops:
  7.2 2.5 constant_dynamic-slice_fusion.1
  13.1 0.9 copy.40
  14.1 0.9 copy.42
  15.1 1.8 copy.54
  17.0 2.9 collective-permute-start
  19.9 1.5 collective-permute-start.1
  21.5 1.0 copy.44
  22.6 32.1 %collective-permute-done.refs_1_ = bf16[384,2048]{1,0:T(8,128)(2,1)} collective-permute-done((bf16[384,2048]{1,0:T(8,128)(2,1)S(1)}, bf16[384,2048]{1,0:T(8,128)(2,1)}, u32[]{:S(2)}, u32[]{:S(2)}) %collective-permute-start) | collective-permute-done | bytes 1572896 | tf_op jit(solution)/shard_map/ppermute | solution.py:205
  54.7 1.2 slice.164
  55.9 1.8 collective-permute-start.2
  57.8 1.2 slice.165
  59.0 1.6 collective-permute-start.3
  61.0 14.0 %collective-permute-done.2.refs_3_ = bf16[192,2048]{1,0:T(8,128)(2,1)S(1)} collective-permute-done((bf16[192,2048]{1,0:T(8,128)(2,1)S(1)}, bf16[192,2048]{1,0:T(8,128)(2,1)S(1)}, u32[]{:S(2)}, u32[]{:S(2)}) %collective-permute-start.2) | collective-permute-done | bytes 786464 | tf_op jit(solution)/shard_map/ppermute | solution.py:205
  75.1 2.5 collective-permute-done.3.refs_4_
  77.6 0.9 dynamic-slice_bitcast_fusion
  79.7 1.0 copy.46
  80.8 1.1 copy-done.7
  82.0 12.4 %shard_map.59 = (bf16[2,2,128,1024]{3,2,1,0:T(8,128)(2,1)S(1)}, f32[4,768,256]{2,1,0:T(8,128)}) custom-call(bf16[384,2048]{1,0:T(8,128)(2,1)S(1)} %bitcast.125, bf16[384,2048]{1,0:T(8,128)(2,1)} %collective-permute-done.refs_1_, bf16[384,2048]{1,0:T(8,128)(2,1)} %collective-permute-done.1.refs_2_, bf16[192,2048]{1,0:T(8,128)(2,1)S(1)} %copy-done.7, ...), custom_call_target="tpu_custom_call" | custom-call | flops 6442450944 | bytes 12582912 | tf_op jit(solution)/shard_map/pallas_call | solution.py:138
  94.4 2.7 bitcast_convert_fusion.6
  97.1 4.2 collective-permute-start.14
  102.3 1.1 copy-done.8
  103.4 12.4 %shard_map.60 = (bf16[2,2,128,1024]{3,2,1,0:T(8,128)(2,1)S(1)}, f32[4,768,256]{2,1,0:T(8,128)}) custom-call(bf16[384,2048]{1,0:T(8,128)(2,1)S(1)} %bitcast.126, bf16[384,2048]{1,0:T(8,128)(2,1)} %collective-permute-done.refs_1_, bf16[384,2048]{1,0:T(8,128)(2,1)} %collective-permute-done.1.refs_2_, bf16[192,2048]{1,0:T(8,128)(2,1)S(1)} %copy-done.8, ...), custom_call_target="tpu_custom_call" | custom-call | flops 6442450944 | bytes 12582912 | tf_op jit(solution)/shard_map/pallas_call | solution.py:138
  115.9 1.0 copy-done.1
  116.8 2.3 bitcast_convert_fusion.4
  119.2 2.0 collective-permute-start.20
  121.9 21.0 %all-gather.13.cloned.1.call-done = bf16[8,384,256]{2,1,0:T(8,128)(2,1)} async-done(((bf16[2,384,256]{2,1,0:T(8,128)(2,1)}), bf16[8,384,256]{2,1,0:T(8,128)(2,1)}) %all-gather.13.cloned.1.call-update) | async-done | bytes 1572880 | tf_op jit(solution)/shard_map/all_gather | solution.py:256
  142.9 1.1 copy-done.9
  144.0 12.5 %shard_map.61 = (bf16[2,2,128,1024]{3,2,1,0:T(8,128)(2,1)S(1)}, f32[4,768,256]{2,1,0:T(8,128)}) custom-call(bf16[384,2048]{1,0:T(8,128)(2,1)S(1)} %bitcast.127, bf16[384,2048]{1,0:T(8,128)(2,1)} %collective-permute-done.refs_1_, bf16[384,2048]{1,0:T(8,128)(2,1)} %collective-permute-done.1.refs_2_, bf16[192,2048]{1,0:T(8,128)(2,1)S(1)} %copy-done.9, ...), custom_call_target="tpu_custom_call" | custom-call | flops 6442450944 | bytes 12582912 | tf_op jit(solution)/shard_map/pallas_call | solution.py:138
  156.5 1.0 copy-done.3
  157.5 2.4 bitcast_convert_fusion.2
  159.8 6.9 %collective-permute-start.26 = (bf16[768,256]{1,0:T(8,128)(2,1)}, bf16[768,256]{1,0:T(8,128)(2,1)}, u32[]{:S(2)}, u32[]{:S(2)}) collective-permute-start(bf16[768,256]{1,0:T(8,128)(2,1)} %get-tuple-element.28), channel_id=1, source_target_pairs={{0,1},{4,5},{8,9},{12,13},{16,17},{20,21},{24,25},{28,29}} | collective-permute-start | bytes 1179656 | tf_op jit(solution)/shard_map/ppermute | solution.py:215
  166.7 22.1 %all-gather.15.cloned.1.call-done = bf16[8,384,256]{2,1,0:T(8,128)(2,1)} async-done(((bf16[2,384,256]{2,1,0:T(8,128)(2,1)}), bf16[8,384,256]{2,1,0:T(8,128)(2,1)}) %all-gather.15.cloned.1.call-update) | async-done | bytes 1572880 | tf_op jit(solution)/shard_map/all_gather | solution.py:256
  188.8 1.1 copy-done.10
  189.9 12.7 %shard_map.62 = (bf16[2,2,128,1024]{3,2,1,0:T(8,128)(2,1)S(1)}, f32[4,768,256]{2,1,0:T(8,128)}) custom-call(bf16[384,2048]{1,0:T(8,128)(2,1)S(1)} %bitcast.128, bf16[384,2048]{1,0:T(8,128)(2,1)} %collective-permute-done.refs_1_, bf16[384,2048]{1,0:T(8,128)(2,1)} %collective-permute-done.1.refs_2_, bf16[192,2048]{1,0:T(8,128)(2,1)S(1)} %copy-done.10, ...), custom_call_target="tpu_custom_call" | custom-call | flops 6442450944 | bytes 12582912 | tf_op jit(solution)/shard_map/pallas_call | solution.py:138
  202.7 1.9 bitcast_convert_fusion
  205.3 1.1 fusion.16
  206.4 4.9 collective-permute-start.32
  211.3 1.1 fusion.11
  212.4 1.3 collective-permute-start.15
  213.8 1.3 fusion.6
  215.1 5.7 collective-permute-done.32
  220.8 4.4 collective-permute-start.21
  226.0 3.2 collective-permute-done.15
  229.2 4.4 collective-permute-start.27
  233.9 3.7 collective-permute-done.21
  237.6 4.4 collective-permute-start.33
  243.0 3.1 collective-permute-done.27
  246.1 4.4 collective-permute-start.16
  251.4 3.1 collective-permute-done.33
  254.5 4.4 collective-permute-start.22
  260.7 1.3 collective-permute-start.19
  262.1 1.3 collective-permute-start.25
  263.5 22.0 %collective-permute-start.28 = (bf16[768,256]{1,0:T(8,128)(2,1)S(1)}, bf16[768,256]{1,0:T(8,128)(2,1)S(1)}, u32[]{:S(2)}, u32[]{:S(2)}) collective-permute-start(bf16[768,256]{1,0:T(8,128)(2,1)S(1)} %get-tuple-element.26), channel_id=1, source_target_pairs={{0,1},{1,2},{2,3},{4,5},{5,6},{6,7},{8,9},{9,10},{10,11},{12,13},{... | collective-permute-start | bytes 1179656 | tf_op jit(solution)/shard_map/ppermute | solution.py:215
  285.6 1.3 collective-permute-start.31
  287.1 3.9 collective-permute-done.25
  291.1 9.2 %collective-permute-start.34 = (bf16[768,256]{1,0:T(8,128)(2,1)S(1)}, bf16[768,256]{1,0:T(8,128)(2,1)S(1)}, u32[]{:S(2)}, u32[]{:S(2)}) collective-permute-start(bf16[768,256]{1,0:T(8,128)(2,1)S(1)} %get-tuple-element.30), channel_id=1, source_target_pairs={{0,1},{1,2},{2,3},{4,5},{5,6},{6,7},{8,9},{9,10},{10,11},{12,13},{... | collective-permute-start | bytes 1179656 | tf_op jit(solution)/shard_map/ppermute | solution.py:215
  300.4 1.5 collective-permute-start.37
  303.7 5.7 collective-permute-done.34
  310.2 3.3 collective-permute-done.37
  316.9 255.3 %shard_map.63 = bf16[2,2,1024,1024]{3,2,1,0:T(8,128)(2,1)} custom-call(bf16[2,2,128,1024]{3,2,1,0:T(8,128)(2,1)} %copy-done, bf16[2,2,128,1024]{3,2,1,0:T(8,128)(2,1)} %copy-done.1, bf16[2,2,128,1024]{3,2,1,0:T(8,128)(2,1)} %copy-done.3, bf16[2,2,128,1024]{3,2,1,0:T(8,128)(2,1)} %copy-done.5, bf16[2,2,128,1024]{3,2,1,0:T(8,128)(2,1)} %collective-permute-done.10.refs_4_, ...), custom_call_target="tpu_custom_call" | custom-call | bytes 16777216 | tf_op jit(solution)/shard_map/pallas_call | solution.py:188
  573.5 1.2 stack.53
  574.7 1.2 stack.54
  575.9 1.5 copy_bitcast_fusion
  577.4 3.6 maximum_select_fusion
  (134 shorter events, 20.1 us)
Async XLA Ops:
  7.2 73.6 %all-gather.9.cloned.1.call-start = ((), (), s32[]{:S(2)}) async-start(), calls=%async_computation | async-start | bytes 1966080 | tf_op jit(solution)/shard_map/all_gather | solution.py:256
  10.5 2.4 collective-permute-start.9
  12.5 1.6 copy-start.19
  14.0 88.2 %all-gather.11.cloned.1.call-start = ((), (), s32[]{:S(2)}) async-start(), calls=%async_computation.1 | async-start | bytes 1966080 | tf_op jit(solution)/shard_map/all_gather | solution.py:256
  15.1 127.8 %all-gather.13.cloned.1.call-start = ((), (), s32[]{:S(2)}) async-start(), calls=%async_computation.2 | async-start | bytes 1966080 | tf_op jit(solution)/shard_map/all_gather | solution.py:256
  17.0 37.7 %collective-permute-start = (bf16[384,2048]{1,0:T(8,128)(2,1)S(1)}, bf16[384,2048]{1,0:T(8,128)(2,1)}, u32[]{:S(2)}, u32[]{:S(2)}) collective-permute-start(bf16[384,2048]{1,0:T(8,128)(2,1)S(1)} %bitcast.122), channel_id=1, source_target_pairs={{0,4},{4,0},{8,12},{12,8},{1,5},{5,1},{9,13},{13,9},{2,6},{6,2},{1... | collective-permute-start | bytes 4718600 | tf_op jit(solution)/shard_map/ppermute | solution.py:205
  19.9 37.9 %collective-permute-start.1 = (bf16[384,2048]{1,0:T(8,128)(2,1)S(1)}, bf16[384,2048]{1,0:T(8,128)(2,1)}, u32[]{:S(2)}, u32[]{:S(2)}) collective-permute-start(bf16[384,2048]{1,0:T(8,128)(2,1)S(1)} %bitcast.123), channel_id=1, source_target_pairs={{0,8},{4,12},{8,0},{12,4},{1,9},{5,13},{9,1},{13,5},{2,10},{6,14},... | collective-permute-start | bytes 4718600 | tf_op jit(solution)/shard_map/ppermute | solution.py:205
  22.5 166.3 %all-gather.15.cloned.1.call-start = ((), (), s32[]{:S(2)}) async-start(), calls=%async_computation.3 | async-start | bytes 1966080 | tf_op jit(solution)/shard_map/all_gather | solution.py:256
  22.5 58.2 %collective-permute-start.4 = (bf16[384,2048]{1,0:T(8,128)(2,1)S(1)}, bf16[384,2048]{1,0:T(8,128)(2,1)}, u32[]{:S(2)}, u32[]{:S(2)}) collective-permute-start(bf16[384,2048]{1,0:T(8,128)(2,1)S(1)} %bitcast.124), channel_id=1, source_target_pairs={{0,16},{16,0},{1,17},{17,1},{2,18},{18,2},{3,19},{19,3},{4,20},{20... | collective-permute-start | bytes 4718600 | tf_op jit(solution)/shard_map/ppermute | solution.py:201
  55.9 24.9 %copy-start.11 = (f32[2]{0:T(128)S(1)}, f32[2]{0:T(128)}, u32[]{:S(2)}) copy-start(f32[2]{0:T(128)} %refs_11_.7) | copy-start | bytes 28
  55.9 19.1 %collective-permute-start.2 = (bf16[192,2048]{1,0:T(8,128)(2,1)S(1)}, bf16[192,2048]{1,0:T(8,128)(2,1)S(1)}, u32[]{:S(2)}, u32[]{:S(2)}) collective-permute-start(bf16[192,2048]{1,0:T(8,128)(2,1)S(1)} %slice.164), channel_id=1, source_target_pairs={{0,8},{4,12},{8,0},{12,4},{1,9},{5,13},{9,1},{13,5},{2,10},{6,14},... | collective-permute-start | bytes 2359304 | tf_op jit(solution)/shard_map/ppermute | solution.py:205
  59.0 18.6 %collective-permute-start.3 = (bf16[192,2048]{1,0:T(8,128)(2,1)S(1)}, bf16[192,2048]{1,0:T(8,128)(2,1)}, u32[]{:S(2)}, u32[]{:S(2)}) collective-permute-start(bf16[192,2048]{1,0:T(8,128)(2,1)S(1)} %slice.165), channel_id=1, source_target_pairs={{0,4},{4,0},{8,12},{12,8},{1,5},{5,1},{9,13},{13,9},{2,6},{6,2},{1... | collective-permute-start | bytes 2359304 | tf_op jit(solution)/shard_map/ppermute | solution.py:205
  60.5 20.2 %collective-permute-start.5 = (bf16[384,2048]{1,0:T(8,128)(2,1)}, bf16[384,2048]{1,0:T(8,128)(2,1)}, u32[]{:S(2)}, u32[]{:S(2)}) collective-permute-start(bf16[384,2048]{1,0:T(8,128)(2,1)} %collective-permute-done.refs_1_), channel_id=1, source_target_pairs={{0,16},{16,0},{1,17},{17,1},{2,18},{18,2},{3,19},{19,3},{4,20},{20... | collective-permute-start | bytes 4718600 | tf_op jit(solution)/shard_map/ppermute | solution.py:201
  60.5 20.2 %collective-permute-start.6 = (bf16[384,2048]{1,0:T(8,128)(2,1)}, bf16[384,2048]{1,0:T(8,128)(2,1)}, u32[]{:S(2)}, u32[]{:S(2)}) collective-permute-start(bf16[384,2048]{1,0:T(8,128)(2,1)} %collective-permute-done.1.refs_2_), channel_id=1, source_target_pairs={{0,16},{16,0},{1,17},{17,1},{2,18},{18,2},{3,19},{19,3},{4,20},{20... | collective-permute-start | bytes 4718600 | tf_op jit(solution)/shard_map/ppermute | solution.py:201
  75.1 5.7 copy-start.6
  75.1 5.7 collective-permute-start.7
  77.6 3.1 collective-permute-start.8
  80.8 1.1 copy-start.7
  94.4 215.0 %copy-start = (bf16[2,2,128,1024]{3,2,1,0:T(8,128)(2,1)}, bf16[2,2,128,1024]{3,2,1,0:T(8,128)(2,1)S(1)}, u32[]{:S(2)}) copy-start(bf16[2,2,128,1024]{3,2,1,0:T(8,128)(2,1)S(1)} %get-tuple-element.10.refs_0_) | copy-start | bytes 3145732
  97.1 107.4 %collective-permute-start.14 = (bf16[768,256]{1,0:T(8,128)(2,1)}, bf16[768,256]{1,0:T(8,128)(2,1)}, u32[]{:S(2)}, u32[]{:S(2)}) collective-permute-start(bf16[768,256]{1,0:T(8,128)(2,1)} %get-tuple-element.20), channel_id=1, source_target_pairs={{0,1},{4,5},{8,9},{12,13},{16,17},{20,21},{24,25},{28,29}} | collective-permute-start | bytes 1179656 | tf_op jit(solution)/shard_map/ppermute | solution.py:215
  101.4 123.9 %collective-permute-start.17 = (bf16[768,256]{1,0:T(8,128)(2,1)}, bf16[768,256]{1,0:T(8,128)(2,1)S(1)}, u32[]{:S(2)}, u32[]{:S(2)}) collective-permute-start(bf16[768,256]{1,0:T(8,128)(2,1)} %get-tuple-element.21), channel_id=1, source_target_pairs={{3,2},{7,6},{11,10},{15,14},{19,18},{23,22},{27,26},{31,30}} | collective-permute-start | bytes 1179656 | tf_op jit(solution)/shard_map/ppermute | solution.py:218
  102.3 1.1 copy-start.8
  115.9 1.0 copy-start.1
  119.2 87.2 %collective-permute-start.20 = (bf16[768,256]{1,0:T(8,128)(2,1)}, bf16[768,256]{1,0:T(8,128)(2,1)}, u32[]{:S(2)}, u32[]{:S(2)}) collective-permute-start(bf16[768,256]{1,0:T(8,128)(2,1)} %get-tuple-element.24), channel_id=1, source_target_pairs={{0,1},{4,5},{8,9},{12,13},{16,17},{20,21},{24,25},{28,29}} | collective-permute-start | bytes 1179656 | tf_op jit(solution)/shard_map/ppermute | solution.py:215
  121.2 112.6 %collective-permute-start.23 = (bf16[768,256]{1,0:T(8,128)(2,1)}, bf16[768,256]{1,0:T(8,128)(2,1)S(1)}, u32[]{:S(2)}, u32[]{:S(2)}) collective-permute-start(bf16[768,256]{1,0:T(8,128)(2,1)} %get-tuple-element.25), channel_id=1, source_target_pairs={{3,2},{7,6},{11,10},{15,14},{19,18},{23,22},{27,26},{31,30}} | collective-permute-start | bytes 1179656 | tf_op jit(solution)/shard_map/ppermute | solution.py:218
  142.9 1.1 copy-start.9
  159.8 52.6 %collective-permute-start.26 = (bf16[768,256]{1,0:T(8,128)(2,1)}, bf16[768,256]{1,0:T(8,128)(2,1)}, u32[]{:S(2)}, u32[]{:S(2)}) collective-permute-start(bf16[768,256]{1,0:T(8,128)(2,1)} %get-tuple-element.28), channel_id=1, source_target_pairs={{0,1},{4,5},{8,9},{12,13},{16,17},{20,21},{24,25},{28,29}} | collective-permute-start | bytes 1179656 | tf_op jit(solution)/shard_map/ppermute | solution.py:215
  188.8 1.1 copy-start.10
  189.9 15.4 %copy-start.13 = (f32[4,768,256]{2,1,0:T(8,128)S(1)}, f32[4,768,256]{2,1,0:T(8,128)}, u32[]{:S(2)}) copy-start(f32[4,768,256]{2,1,0:T(8,128)} %get-tuple-element.14) | copy-start | bytes 9437188
  202.7 31.2 %copy-start.5 = (bf16[2,2,128,1024]{3,2,1,0:T(8,128)(2,1)}, bf16[2,2,128,1024]{3,2,1,0:T(8,128)(2,1)S(1)}, u32[]{:S(2)}) copy-start(bf16[2,2,128,1024]{3,2,1,0:T(8,128)(2,1)S(1)} %get-tuple-element.13.refs_3_) | copy-start | bytes 3145732
  202.7 8.6 %copy-start.14 = (f32[4,768,256]{2,1,0:T(8,128)S(1)}, f32[4,768,256]{2,1,0:T(8,128)}, u32[]{:S(2)}) copy-start(f32[4,768,256]{2,1,0:T(8,128)} %get-tuple-element.15) | copy-start | bytes 9437188
  204.6 37.7 %collective-permute-start.29 = (bf16[768,256]{1,0:T(8,128)(2,1)}, bf16[768,256]{1,0:T(8,128)(2,1)S(1)}, u32[]{:S(2)}, u32[]{:S(2)}) collective-permute-start(bf16[768,256]{1,0:T(8,128)(2,1)} %get-tuple-element.29), channel_id=1, source_target_pairs={{3,2},{7,6},{11,10},{15,14},{19,18},{23,22},{27,26},{31,30}} | collective-permute-start | bytes 1179656 | tf_op jit(solution)/shard_map/ppermute | solution.py:218
  206.4 18.8 %copy-start.12 = (f32[4,768,256]{2,1,0:T(8,128)S(1)}, f32[4,768,256]{2,1,0:T(8,128)}, u32[]{:S(2)}) copy-start(f32[4,768,256]{2,1,0:T(8,128)} %get-tuple-element.17) | copy-start | bytes 9437188
  206.4 14.4 %collective-permute-start.32 = (bf16[768,256]{1,0:T(8,128)(2,1)S(1)}, bf16[768,256]{1,0:T(8,128)(2,1)S(1)}, u32[]{:S(2)}, u32[]{:S(2)}) collective-permute-start(bf16[768,256]{1,0:T(8,128)(2,1)S(1)} %get-tuple-element.32), channel_id=1, source_target_pairs={{0,1},{4,5},{8,9},{12,13},{16,17},{20,21},{24,25},{28,29}} | collective-permute-start | bytes 1179656 | tf_op jit(solution)/shard_map/ppermute | solution.py:215
  212.4 16.8 %collective-permute-start.15 = (bf16[768,256]{1,0:T(8,128)(2,1)S(1)}, bf16[768,256]{1,0:T(8,128)(2,1)S(1)}, u32[]{:S(2)}, u32[]{:S(2)}) collective-permute-start(bf16[768,256]{1,0:T(8,128)(2,1)S(1)} %fusion.16), channel_id=1, source_target_pairs={{0,1},{1,2},{4,5},{5,6},{8,9},{9,10},{12,13},{13,14},{16,17},{17,1... | collective-permute-start | bytes 1179656 | tf_op jit(solution)/shard_map/ppermute | solution.py:215
  220.8 16.9 %collective-permute-start.21 = (bf16[768,256]{1,0:T(8,128)(2,1)S(1)}, bf16[768,256]{1,0:T(8,128)(2,1)S(1)}, u32[]{:S(2)}, u32[]{:S(2)}) collective-permute-start(bf16[768,256]{1,0:T(8,128)(2,1)S(1)} %fusion.11), channel_id=1, source_target_pairs={{0,1},{1,2},{4,5},{5,6},{8,9},{9,10},{12,13},{13,14},{16,17},{17,1... | collective-permute-start | bytes 1179656 | tf_op jit(solution)/shard_map/ppermute | solution.py:215
  225.3 25.4 %collective-permute-start.35 = (bf16[768,256]{1,0:T(8,128)(2,1)S(1)}, bf16[768,256]{1,0:T(8,128)(2,1)S(1)}, u32[]{:S(2)}, u32[]{:S(2)}) collective-permute-start(bf16[768,256]{1,0:T(8,128)(2,1)S(1)} %get-tuple-element.33), channel_id=1, source_target_pairs={{3,2},{7,6},{11,10},{15,14},{19,18},{23,22},{27,26},{31,30}} | collective-permute-start | bytes 1179656 | tf_op jit(solution)/shard_map/ppermute | solution.py:218
  229.2 16.9 %collective-permute-start.27 = (bf16[768,256]{1,0:T(8,128)(2,1)S(1)}, bf16[768,256]{1,0:T(8,128)(2,1)S(1)}, u32[]{:S(2)}, u32[]{:S(2)}) collective-permute-start(bf16[768,256]{1,0:T(8,128)(2,1)S(1)} %fusion.6), channel_id=1, source_target_pairs={{0,1},{1,2},{4,5},{5,6},{8,9},{9,10},{12,13},{13,14},{16,17},{17,1... | collective-permute-start | bytes 1179656 | tf_op jit(solution)/shard_map/ppermute | solution.py:215
  233.9 16.6 %copy-start.15 = (f32[4,768,256]{2,1,0:T(8,128)S(1)}, f32[4,768,256]{2,1,0:T(8,128)}, u32[]{:S(2)}) copy-start(f32[4,768,256]{2,1,0:T(8,128)} %get-tuple-element.16) | copy-start | bytes 9437188
  233.9 80.6 %collective-permute-start.13 = (bf16[2,2,128,1024]{3,2,1,0:T(8,128)(2,1)S(1)}, bf16[2,2,128,1024]{3,2,1,0:T(8,128)(2,1)S(1)}, u32[]{:S(2)}, u32[]{:S(2)}) collective-permute-start(bf16[2,2,128,1024]{3,2,1,0:T(8,128)(2,1)S(1)} %get-tuple-element.13.refs_3_), channel_id=1, source_target_pairs={{0,16},{16,0},{1,17},{17,1},{2,18},{18,2},{3,19},{19,3},{4,20},{20... | collective-permute-start | bytes 3145736 | tf_op jit(solution)/shard_map/ppermute | solution.py:201
  237.6 16.9 %collective-permute-start.33 = (bf16[768,256]{1,0:T(8,128)(2,1)S(1)}, bf16[768,256]{1,0:T(8,128)(2,1)S(1)}, u32[]{:S(2)}, u32[]{:S(2)}) collective-permute-start(bf16[768,256]{1,0:T(8,128)(2,1)S(1)} %fusion.1), channel_id=1, source_target_pairs={{0,1},{1,2},{4,5},{5,6},{8,9},{9,10},{12,13},{13,14},{16,17},{17,1... | collective-permute-start | bytes 1179656 | tf_op jit(solution)/shard_map/ppermute | solution.py:215
  242.3 16.8 %collective-permute-start.18 = (bf16[768,256]{1,0:T(8,128)(2,1)S(1)}, bf16[768,256]{1,0:T(8,128)(2,1)S(1)}, u32[]{:S(2)}, u32[]{:S(2)}) collective-permute-start(bf16[768,256]{1,0:T(8,128)(2,1)S(1)} %get-tuple-element.19), channel_id=1, source_target_pairs={{3,2},{2,1},{7,6},{6,5},{11,10},{10,9},{15,14},{14,13},{19,18},{18... | collective-permute-start | bytes 1179656 | tf_op jit(solution)/shard_map/ppermute | solution.py:218
  246.1 17.5 %collective-permute-start.16 = (bf16[768,256]{1,0:T(8,128)(2,1)S(1)}, bf16[768,256]{1,0:T(8,128)(2,1)S(1)}, u32[]{:S(2)}, u32[]{:S(2)}) collective-permute-start(bf16[768,256]{1,0:T(8,128)(2,1)S(1)} %get-tuple-element.18), channel_id=1, source_target_pairs={{0,1},{1,2},{2,3},{4,5},{5,6},{6,7},{8,9},{9,10},{10,11},{12,13},{... | collective-permute-start | bytes 1179656 | tf_op jit(solution)/shard_map/ppermute | solution.py:215
  250.7 9.2 %collective-permute-start.24 = (bf16[768,256]{1,0:T(8,128)(2,1)S(1)}, bf16[768,256]{1,0:T(8,128)(2,1)S(1)}, u32[]{:S(2)}, u32[]{:S(2)}) collective-permute-start(bf16[768,256]{1,0:T(8,128)(2,1)S(1)} %get-tuple-element.23), channel_id=1, source_target_pairs={{3,2},{2,1},{7,6},{6,5},{11,10},{10,9},{15,14},{14,13},{19,18},{18... | collective-permute-start | bytes 1179656 | tf_op jit(solution)/shard_map/ppermute | solution.py:218
  254.5 32.5 %collective-permute-start.22 = (bf16[768,256]{1,0:T(8,128)(2,1)S(1)}, bf16[768,256]{1,0:T(8,128)(2,1)S(1)}, u32[]{:S(2)}, u32[]{:S(2)}) collective-permute-start(bf16[768,256]{1,0:T(8,128)(2,1)S(1)} %get-tuple-element.22), channel_id=1, source_target_pairs={{0,1},{1,2},{2,3},{4,5},{5,6},{6,7},{8,9},{9,10},{10,11},{12,13},{... | collective-permute-start | bytes 1179656 | tf_op jit(solution)/shard_map/ppermute | solution.py:215
  259.1 1.6 collective-permute-start.30
  259.9 2.2 collective-permute-start.36
  260.7 24.9 %collective-permute-start.19 = (bf16[768,256]{1,0:T(8,128)(2,1)S(1)}, bf16[768,256]{1,0:T(8,128)(2,1)S(1)}, u32[]{:S(2)}, u32[]{:S(2)}) collective-permute-start(bf16[768,256]{1,0:T(8,128)(2,1)S(1)} %fusion.15), channel_id=1, source_target_pairs={{3,2},{2,1},{1,0},{7,6},{6,5},{5,4},{11,10},{10,9},{9,8},{15,14},{... | collective-permute-start | bytes 1179656 | tf_op jit(solution)/shard_map/ppermute | solution.py:218
  262.1 28.9 %collective-permute-start.25 = (bf16[768,256]{1,0:T(8,128)(2,1)S(1)}, bf16[768,256]{1,0:T(8,128)(2,1)S(1)}, u32[]{:S(2)}, u32[]{:S(2)}) collective-permute-start(bf16[768,256]{1,0:T(8,128)(2,1)S(1)} %fusion.10), channel_id=1, source_target_pairs={{3,2},{2,1},{1,0},{7,6},{6,5},{5,4},{11,10},{10,9},{9,8},{15,14},{... | collective-permute-start | bytes 1179656 | tf_op jit(solution)/shard_map/ppermute | solution.py:218
  263.5 23.5 %copy-start.4 = (bf16[2,2,128,1024]{3,2,1,0:T(8,128)(2,1)S(1)}, bf16[2,2,128,1024]{3,2,1,0:T(8,128)(2,1)}, u32[]{:S(2)}) copy-start(bf16[2,2,128,1024]{3,2,1,0:T(8,128)(2,1)} %copy-done.3) | copy-start | bytes 3145732
  263.5 27.5 %copy-start.2 = (bf16[2,2,128,1024]{3,2,1,0:T(8,128)(2,1)S(1)}, bf16[2,2,128,1024]{3,2,1,0:T(8,128)(2,1)}, u32[]{:S(2)}) copy-start(bf16[2,2,128,1024]{3,2,1,0:T(8,128)(2,1)} %copy-done.1) | copy-start | bytes 3145732
  263.5 27.6 %collective-permute-start.28 = (bf16[768,256]{1,0:T(8,128)(2,1)S(1)}, bf16[768,256]{1,0:T(8,128)(2,1)S(1)}, u32[]{:S(2)}, u32[]{:S(2)}) collective-permute-start(bf16[768,256]{1,0:T(8,128)(2,1)S(1)} %get-tuple-element.26), channel_id=1, source_target_pairs={{0,1},{1,2},{2,3},{4,5},{5,6},{6,7},{8,9},{9,10},{10,11},{12,13},{... | collective-permute-start | bytes 1179656 | tf_op jit(solution)/shard_map/ppermute | solution.py:215
  285.6 14.8 %collective-permute-start.31 = (bf16[768,256]{1,0:T(8,128)(2,1)S(1)}, bf16[768,256]{1,0:T(8,128)(2,1)S(1)}, u32[]{:S(2)}, u32[]{:S(2)}) collective-permute-start(bf16[768,256]{1,0:T(8,128)(2,1)S(1)} %fusion.5), channel_id=1, source_target_pairs={{3,2},{2,1},{1,0},{7,6},{6,5},{5,4},{11,10},{10,9},{9,8},{15,14},{... | collective-permute-start | bytes 1179656 | tf_op jit(solution)/shard_map/ppermute | solution.py:218
  287.0 28.0 %collective-permute-start.12 = (bf16[2,2,128,1024]{3,2,1,0:T(8,128)(2,1)S(1)}, bf16[2,2,128,1024]{3,2,1,0:T(8,128)(2,1)S(1)}, u32[]{:S(2)}, u32[]{:S(2)}) collective-permute-start(bf16[2,2,128,1024]{3,2,1,0:T(8,128)(2,1)S(1)} %copy-done.4), channel_id=1, source_target_pairs={{0,16},{16,0},{1,17},{17,1},{2,18},{18,2},{3,19},{19,3},{4,20},{20... | collective-permute-start | bytes 3145736 | tf_op jit(solution)/shard_map/ppermute | solution.py:201
  291.0 24.1 %collective-permute-start.11 = (bf16[2,2,128,1024]{3,2,1,0:T(8,128)(2,1)S(1)}, bf16[2,2,128,1024]{3,2,1,0:T(8,128)(2,1)S(1)}, u32[]{:S(2)}, u32[]{:S(2)}) collective-permute-start(bf16[2,2,128,1024]{3,2,1,0:T(8,128)(2,1)S(1)} %copy-done.2), channel_id=1, source_target_pairs={{0,16},{16,0},{1,17},{17,1},{2,18},{18,2},{3,19},{19,3},{4,20},{20... | collective-permute-start | bytes 3145736 | tf_op jit(solution)/shard_map/ppermute | solution.py:201
  291.1 18.3 %collective-permute-start.34 = (bf16[768,256]{1,0:T(8,128)(2,1)S(1)}, bf16[768,256]{1,0:T(8,128)(2,1)S(1)}, u32[]{:S(2)}, u32[]{:S(2)}) collective-permute-start(bf16[768,256]{1,0:T(8,128)(2,1)S(1)} %get-tuple-element.30), channel_id=1, source_target_pairs={{0,1},{1,2},{2,3},{4,5},{5,6},{6,7},{8,9},{9,10},{10,11},{12,13},{... | collective-permute-start | bytes 1179656 | tf_op jit(solution)/shard_map/ppermute | solution.py:215
  300.4 13.1 %collective-permute-start.37 = (bf16[768,256]{1,0:T(8,128)(2,1)S(1)}, bf16[768,256]{1,0:T(8,128)(2,1)S(1)}, u32[]{:S(2)}, u32[]{:S(2)}) collective-permute-start(bf16[768,256]{1,0:T(8,128)(2,1)S(1)} %fusion), channel_id=1, source_target_pairs={{3,2},{2,1},{1,0},{7,6},{6,5},{5,4},{11,10},{10,9},{9,8},{15,14},{... | collective-permute-start | bytes 1179656 | tf_op jit(solution)/shard_map/ppermute | solution.py:218
  309.4 7.5 %collective-permute-start.10 = (bf16[2,2,128,1024]{3,2,1,0:T(8,128)(2,1)S(1)}, bf16[2,2,128,1024]{3,2,1,0:T(8,128)(2,1)}, u32[]{:S(2)}, u32[]{:S(2)}) collective-permute-start(bf16[2,2,128,1024]{3,2,1,0:T(8,128)(2,1)S(1)} %get-tuple-element.10.refs_0_), channel_id=1, source_target_pairs={{0,16},{16,0},{1,17},{17,1},{2,18},{18,2},{3,19},{19,3},{4,20},{20... | collective-permute-start | bytes 3145736 | tf_op jit(solution)/shard_map/ppermute | solution.py:201
  313.5 259.5 %collective-permute-start.38 = (f32[384,256]{1,0:T(8,128)}, f32[384,256]{1,0:T(8,128)S(1)}, u32[]{:S(2)}, u32[]{:S(2)}) collective-permute-start(f32[384,256]{1,0:T(8,128)} %get-tuple-element.37), channel_id=1, source_target_pairs={{0,16},{16,0},{1,17},{17,1},{2,18},{18,2},{3,19},{19,3},{4,20},{20... | collective-permute-start | bytes 1179656 | tf_op jit(solution)/shard_map/ppermute | solution.py:201
  314.5 1.0 copy-start.16
  314.5 258.8 %collective-permute-start.39 = (f32[384,256]{1,0:T(8,128)}, f32[384,256]{1,0:T(8,128)S(1)}, u32[]{:S(2)}, u32[]{:S(2)}) collective-permute-start(f32[384,256]{1,0:T(8,128)} %get-tuple-element.39), channel_id=1, source_target_pairs={{0,16},{16,0},{1,17},{17,1},{2,18},{18,2},{3,19},{19,3},{4,20},{20... | collective-permute-start | bytes 1179656 | tf_op jit(solution)/shard_map/ppermute | solution.py:201
  315.0 1.0 copy-start.17
  315.0 258.5 %collective-permute-start.40 = (f32[384,256]{1,0:T(8,128)}, f32[384,256]{1,0:T(8,128)}, u32[]{:S(2)}, u32[]{:S(2)}) collective-permute-start(f32[384,256]{1,0:T(8,128)} %get-tuple-element.41), channel_id=1, source_target_pairs={{0,16},{16,0},{1,17},{17,1},{2,18},{18,2},{3,19},{19,3},{4,20},{20... | collective-permute-start | bytes 1179656 | tf_op jit(solution)/shard_map/ppermute | solution.py:201
  316.4 258.3 %collective-permute-start.41 = (f32[384,256]{1,0:T(8,128)}, f32[384,256]{1,0:T(8,128)}, u32[]{:S(2)}, u32[]{:S(2)}) collective-permute-start(f32[384,256]{1,0:T(8,128)} %get-tuple-element.43), channel_id=1, source_target_pairs={{0,16},{16,0},{1,17},{17,1},{2,18},{18,2},{3,19},{19,3},{4,20},{20... | collective-permute-start | bytes 1179656 | tf_op jit(solution)/shard_map/ppermute | solution.py:201
  (2 other events, 1.9 us)
Sparse Core Ops, SparseCore 0:
  14.1 39.7 all-gather.8
  56.0 35.9 all-gather.10
  93.6 49.2 all-gather.12
  144.3 44.4 all-gather.14

commit v2 on v1

v2 whole, which is shorter than its diff:
```python
import functools

import jax
import jax.numpy as jnp
from jax import lax
from jax.experimental import pallas as pl
from jax.experimental.pallas import tpu as pltpu
from jax.sharding import PartitionSpec as P


def make_amplitudes(coulomb, occ_energy, virt_first, virt_second):
    denominator = (
        occ_energy[:, None, None, None]
        + occ_energy[None, :, None, None]
        - virt_first[None, None, :, None]
        - virt_second[None, None, None, :]
    )
    return ((2.0 * coulomb - jnp.transpose(coulomb, (1, 0, 2, 3))) / denominator).astype(
        jnp.bfloat16
    )


def general(bra_factor, ket_factor, occ_energy, virt_energy):
    a_width = bra_factor.shape[2]
    b_width = ket_factor.shape[2]
    ket_whole = lax.all_gather(ket_factor, "row", axis=0, tiled=True)
    row_index = lax.axis_index("row")
    col_index = lax.axis_index("col")
    virt_first = lax.dynamic_slice_in_dim(virt_energy, row_index * a_width, a_width, 0)
    virt_second = lax.dynamic_slice_in_dim(virt_energy, col_index * b_width, b_width, 0)
    partial_sum = jnp.einsum(
        "qia,qjb->ijab",
        lax.all_gather(bra_factor, "col", axis=0, tiled=True),
        ket_whole,
        preferred_element_type=jnp.float32,
    )
    batch_count = lax.axis_size("occ")
    pad_rows = (batch_count - a_width % batch_count) % batch_count
    padded = jnp.pad(partial_sum, ((0, 0), (0, 0), (0, pad_rows), (0, 0)))
    share_sum = lax.psum_scatter(padded, "occ", scatter_dimension=2, tiled=True)
    share_len = share_sum.shape[2]
    energy_padded = jnp.pad(virt_first, (0, pad_rows), constant_values=1.0)
    energy_share = lax.dynamic_slice_in_dim(
        energy_padded, lax.axis_index("occ") * share_len, share_len, 0
    )
    share_amps = make_amplitudes(share_sum, occ_energy, energy_share, virt_second)
    collected = lax.all_gather(share_amps, "occ", axis=2, tiled=True)
    amplitudes = collected[:, :, :a_width, :]
    gamma = lax.psum_scatter(
        jnp.einsum("ijab,qjb->qia", amplitudes, ket_whole, preferred_element_type=jnp.float32),
        "col",
        scatter_dimension=0,
        tiled=True,
    )
    return (amplitudes, gamma)


CHUNKS = 4
GROUPS = 4


def chunk_kernel(pieces, cols, steps, chunk, *refs):
    refs = list(refs)
    take = lambda count: [refs.pop(0) for _ in range(count)]
    ket = take(2 * len(pieces))
    (bra,) = take(1)
    ups, downs = take(cols - 1), take(cols - 1)
    occ_ref, first_ref, second_ref = take(3)
    if chunk:
        take(2)
    whole_ref, half_ref, share_ref, up_ref, down_ref = take(5)
    kv, bv, bt, t2, amps, ket_sem, bra_sem, out_sem = refs
    width = first_ref.shape[0]
    span = second_ref.shape[1]
    part = span // GROUPS
    batch = bra.shape[3]
    here_row, here_col = lax.axis_index("row"), lax.axis_index("col")
    me = lax.axis_index("occ")

    def bra_copies(source, place, home, slot):
        return [
            pltpu.make_async_copy(
                source.at[place, q, i],
                bv.at[home, pl.ds(q * batch, batch), pl.ds(i * width, width)],
                bra_sem.at[slot, q, i],
            )
            for q in range(2)
            for i in range(2)
        ]

    for copy in bra_copies(bra, chunk, here_col, 0):
        copy.start()
    for d in range(1, cols):
        home = lax.rem(here_col + cols - d, cols)

        @pl.when(here_col >= d)
        def _():
            for copy in bra_copies(ups[d - 1], steps[d - 1], home, d):
                copy.start()

        @pl.when(here_col < d)
        def _():
            for copy in bra_copies(downs[cols - 1 - d], steps[cols - 1 - d], home, d):
                copy.start()

    copies = []
    for group in range(GROUPS):
        of_group = []
        for q in range(2):
            for index, (offset, begin, rows) in enumerate(pieces):
                home = lax.bitwise_xor(here_row, offset)
                to_row = pl.multiple_of(home * (2 * batch) + q * batch + begin, 16)
                for j in range(2):
                    columns = pl.ds(j * span + group * part, part)
                    copy = pltpu.make_async_copy(
                        ket[q * len(pieces) + index].at[:, columns],
                        kv.at[pl.ds(to_row, rows), columns],
                        ket_sem.at[group, q, index, j],
                    )
                    copy.start()
                    of_group.append(copy)
        copies.append(of_group)
    for d in range(cols):
        home = lax.rem(here_col + cols - d, cols)
        for copy in bra_copies(bra, chunk, home, d):
            copy.wait()
    for d in range(cols):
        bt[:, d * 2 * batch : (d + 1) * 2 * batch] = bv[d].T
    for group in range(GROUPS):
        for copy in copies[group]:
            copy.wait()
        tile = [
            jnp.dot(
                bt[...],
                kv[:, j * span + group * part : j * span + (group + 1) * part],
                preferred_element_type=jnp.float32,
            )
            for j in range(2)
        ]
        second = second_ref[:, group * part : (group + 1) * part]
        for i in range(2):
            for j in range(2):
                direct = tile[j][i * width : (i + 1) * width, :]
                exchange = tile[i][j * width : (j + 1) * width, :]
                denominator = ((occ_ref[i] + occ_ref[j]) - first_ref[...]) - second
                block = ((2.0 * direct - exchange) / denominator).astype(jnp.bfloat16)
                amps[i, j, :, group * part : (group + 1) * part] = block
                t2[
                    i * width : (i + 1) * width,
                    j * span + group * part : j * span + (group + 1) * part,
                ] = block
    half = half_ref.shape[2]
    at = pl.multiple_of(me * half + chunk * width, 16)
    outs = [
        pltpu.make_async_copy(amps, whole_ref.at[:, :, pl.ds(at, width), :], out_sem.at[0]),
        pltpu.make_async_copy(
            amps, half_ref.at[:, :, pl.ds(chunk * width, width), :], out_sem.at[1]
        ),
    ]
    for copy in outs:
        copy.start()
    for t in range(cols):
        home = lax.rem(here_col + t, cols)
        rows = pl.ds(pl.multiple_of(home * (2 * batch), 16), 2 * batch)
        share = lax.dot_general(
            kv[rows, :],
            t2[...],
            (((1,), (1,)), ((), ())),
            preferred_element_type=jnp.float32,
        )
        share_ref[t] = share
        if t == 1:
            down_ref[...] = share.astype(jnp.bfloat16)
        if t == cols - 1:
            up_ref[...] = share.astype(jnp.bfloat16)
    for copy in outs:
        copy.wait()


def run_chunk(chunk, ket, pieces, bra, ups, downs, steps, energies, held):
    _, _, _, batch, width = bra.shape
    cols = len(ups) + 1
    occ_energy, first, second = energies
    span = second.shape[1]
    half = width * CHUNKS
    total = cols * 2 * batch
    flops = 2 * 2 * total * 2 * width * 2 * span
    ins = [*ket, bra, *ups, *downs]
    any_space = pl.BlockSpec(memory_space=pl.ANY)
    in_vmem = pl.BlockSpec(memory_space=pltpu.VMEM)
    return pl.pallas_call(
        functools.partial(chunk_kernel, pieces, cols, steps, chunk),
        out_shape=(
            jax.ShapeDtypeStruct((2, 2, 2 * half, span), jnp.bfloat16),
            jax.ShapeDtypeStruct((2, 2, half, span), jnp.bfloat16),
            jax.ShapeDtypeStruct((cols, 2 * batch, 2 * width), jnp.float32),
            jax.ShapeDtypeStruct((2 * batch, 2 * width), jnp.bfloat16),
            jax.ShapeDtypeStruct((2 * batch, 2 * width), jnp.bfloat16),
        ),
        in_specs=[any_space] * len(ins)
        + [pl.BlockSpec(memory_space=pltpu.SMEM), in_vmem, in_vmem]
        + [any_space] * len(held),
        out_specs=(any_space, any_space, in_vmem, in_vmem, in_vmem),
        scratch_shapes=[
            pltpu.VMEM((total, 2 * span), jnp.bfloat16),
            pltpu.VMEM((cols, 2 * batch, 2 * width), jnp.bfloat16),
            pltpu.VMEM((2 * width, total), jnp.bfloat16),
            pltpu.VMEM((2 * width, 2 * span), jnp.bfloat16),
            pltpu.VMEM((2, 2, width, span), jnp.bfloat16),
            pltpu.SemaphoreType.DMA((GROUPS, 2, len(pieces), 2)),
            pltpu.SemaphoreType.DMA((cols, 2, 2)),
            pltpu.SemaphoreType.DMA((2,)),
        ],
        input_output_aliases={len(ins) + 3 + n: n for n in range(len(held))},
        compiler_params=pltpu.CompilerParams(vmem_limit_bytes=48 * 2**20),
        cost_estimate=pl.CostEstimate(
            flops=flops, bytes_accessed=total * 2 * span * 2, transcendentals=0
        ),
    )(*ins, occ_energy, first, second, *held)


def place_kernel(other, _, out, buffer, sems):
    half = other.shape[2]
    at = pl.multiple_of((1 - lax.axis_index("occ")) * half, 16)
    blocks = [(i, j) for i in range(2) for j in range(2)]
    reads = [
        pltpu.make_async_copy(other.at[i, j], buffer.at[i, j], sems.at[0, i, j]) for i, j in blocks
    ]
    writes = [
        pltpu.make_async_copy(
            buffer.at[i, j], out.at[i, j, pl.ds(at, half), :], sems.at[1, i, j]
        )
        for i, j in blocks
    ]
    for copy in reads:
        copy.start()
    for read, write in zip(reads, writes):
        read.wait()
        write.start()
    for copy in writes:
        copy.wait()


def place(other, whole):
    any_space = pl.BlockSpec(memory_space=pl.ANY)
    return pl.pallas_call(
        place_kernel,
        out_shape=jax.ShapeDtypeStruct(whole.shape, whole.dtype),
        in_specs=[any_space, any_space],
        out_specs=any_space,
        scratch_shapes=[
            pltpu.VMEM(other.shape, other.dtype),
            pltpu.SemaphoreType.DMA((2, 2, 2)),
        ],
        input_output_aliases={1: 0},
        compiler_params=pltpu.CompilerParams(vmem_limit_bytes=16 * 2**20),
        cost_estimate=pl.CostEstimate(
            flops=0, bytes_accessed=4 * other.size, transcendentals=0
        ),
    )(other, whole)


def swap(x):
    return lax.ppermute(x, "occ", [(0, 1), (1, 0)])


def planar(x, offset):
    return lax.ppermute(x, "row", [(r, r ^ offset) for r in range(4)])


def hop_up(x, cols, first=0, last=None):
    last = cols - 1 if last is None else last
    return lax.ppermute(x, "col", [(c, c + 1) for c in range(first, last)])


def hop_down(x, cols, first=0, last=None):
    last = cols - 1 if last is None else last
    return lax.ppermute(x, "col", [(cols - 1 - c, cols - 2 - c) for c in range(first, last)])


def both(*arrays):
    return lax.optimization_barrier(arrays)


def planned(bra_factor, ket_factor, occ_energy, virt_energy):
    batch, _, a_width = bra_factor.shape
    b_width = ket_factor.shape[2]
    half = a_width // 2
    width = half // CHUNKS
    cols = lax.axis_size("col")
    me, row_index, col_index = (lax.axis_index(name) for name in ("occ", "row", "col"))

    ket_own = ket_factor.reshape(batch, 2 * b_width)
    ket_x = planar(ket_own, 1)
    ket_y = planar(ket_own, 2)
    cut = batch // 2
    ket_far_y = planar(ket_x[:cut], 2)
    ket_far_x = planar(ket_y[cut:], 1)
    mine = [ket_own, ket_x, ket_y, ket_far_y, ket_far_x]
    pieces = ((0, 0, batch), (1, 0, batch), (2, 0, batch), (3, 0, cut), (3, cut, batch - cut))
    ket = mine + [swap(piece) for piece in mine]

    bra_plain = both(bra_factor.transpose(1, 0, 2))[0]

    def rows_of(side):
        part = lax.dynamic_slice_in_dim(bra_plain, side * half, half, 2)
        return part.reshape(2, batch, CHUNKS, width).transpose(2, 0, 1, 3)

    bra = jnp.stack([rows_of(me), swap(rows_of(1 - me))], axis=1)

    first_up, first_down = hop_up(bra[:1], cols), hop_down(bra[:1], cols)
    rest_up, rest_down = hop_up(bra[1:], cols), hop_down(bra[1:], cols)
    arrived = {0: ([first_up], [first_down])}
    for k in range(1, CHUNKS):
        arrived[k] = ([rest_up[k - 1 : k]], [rest_down[k - 1 : k]])

    def pass_on(k):
        ups, downs = arrived[k]
        for step in range(1, cols - 1):
            ups.append(hop_up(ups[-1], cols, first=step))
            downs.append(hop_down(downs[-1], cols, first=step))

    for k in range(CHUNKS):
        pass_on(k)

    second = lax.dynamic_slice_in_dim(virt_energy, col_index * b_width, b_width, 0)[None, :]
    first_all = lax.dynamic_slice_in_dim(virt_energy, row_index * a_width + me * half, half, 0)
    first_all = first_all[:, None]

    held = ()
    sums = {}
    shares = {}

    def step_sum(k, step):
        if step == 0:
            send_up, send_down = shares[k][1:]
        else:
            share = shares[k][0]
            up, down = sums[k]
            send_up = (share[cols - 1 - step] + up.astype(jnp.float32)).astype(jnp.bfloat16)
            send_down = (share[step + 1] + down.astype(jnp.float32)).astype(jnp.bfloat16)
        sums[k] = (hop_up(send_up, cols, last=step + 1), hop_down(send_down, cols, last=step + 1))

    ticks = CHUNKS + cols - 2
    for tick in range(ticks):
        if tick < CHUNKS:
            k = tick
            ups, downs = arrived[k]
            if k >= 2:
                older = [n for n in range(k - 1) if n in sums and n >= k - cols]
                flat = [x for n in older for x in sums[n]]
                tied = both(ups[0], *flat)
                ups = [tied[0], *ups[1:]]
                flat = tied[1:]
                for index, n in enumerate(older):
                    sums[n] = (flat[2 * index], flat[2 * index + 1])
            first = first_all[k * width : (k + 1) * width]
            steps = [0] * (cols - 1)
            *held, share, send_up, send_down = run_chunk(
                k, ket, pieces, bra, ups, downs, steps, (occ_energy, first, second), held
            )
            shares[k] = (share, send_up, send_down)
        for step in range(cols - 2, -1, -1):
            if 0 <= tick - step < CHUNKS:
                step_sum(tick - step, step)

    whole, mine_half = held
    amplitudes = place(swap(mine_half), whole)

    totals = []
    for k in range(CHUNKS):
        up, down = sums[k]
        totals.append(shares[k][0][0] + up.astype(jnp.float32) + down.astype(jnp.float32))

    def gathered(parts):
        whole = jnp.stack(parts).reshape(CHUNKS, batch, 2, width)
        return whole.transpose(1, 2, 0, 3).reshape(batch, 2, half)

    kept = gathered([total[:batch] for total in totals])
    received = gathered([swap(total[batch:]) for total in totals])
    gamma = jnp.where(
        me == 0,
        jnp.concatenate([kept, received], axis=2),
        jnp.concatenate([received, kept], axis=2),
    )
    return (amplitudes, gamma)


def solution(mesh):
    sizes = mesh.shape

    def on_device(bra_factor, ket_factor, occ_energy, virt_energy):
        fits = (
            sizes["occ"] == 2
            and sizes["row"] == 4
            and sizes["col"] > 1
            and bra_factor.shape[2] % (256 * CHUNKS) == 0
            and ket_factor.shape[2] % 512 == 0
            and bra_factor.shape[0] % 128 == 0
        )
        body = planned if fits else general
        return body(bra_factor, ket_factor, occ_energy, virt_energy)

    placed = (P(("occ", "col"), None, "row"), P(("occ", "row"), None, "col"), P(), P())
    return jax.shard_map(
        on_device,
        mesh=mesh,
        in_specs=placed,
        out_specs=(P(None, None, "row", "col"), P(("occ", "col"), None, "row")),
        check_vma=False,
    )
```

time: 597 us -> 306 us (0.51)
  Pallas kernels: 305 us -> 58.4 us
  waiting for transfers between devices: 124 us -> 86.7 us
  between operations: 15.1 us -> 2.14 us
  other arithmetic: 10.5 us -> 21.8 us
  local copies, waits for them, and re-layouts: 38.9 us -> 29.6 us
  starting transfers between devices: 94 us -> 102 us
    pallas_call x5, Pallas kernels: 305 us -> 58.4 us  [the longest x4 55.1 us: run_chunk(): pl.pallas_call(functools.partial(chunk_kernel, pieces, cols, steps, chunk...]
    ppermute x24 -> x44, waiting for transfers between devices: 31.7 us -> 86.7 us  [the longest x22 59.9 us: hop_down(): lax.ppermute(x, 'col', [(cols - 1 - c, cols - 2 - c) for c in range(first...]
    ppermute x4, waiting for transfers between devices: 48.7 us -> 0.01 us  [planar(): return lax.ppermute(x, 'row', [(r, r ^ offset) for r in range(4)])]
    all_gather x4 -> x0, waiting for transfers between devices: 43.1 us -> none  [planned(): bra = lax.all_gather(jnp.stack([bra_own[k], bra_other[k]]), 'col', axis=0)]
    ppermute x24 -> x44, starting transfers between devices: 83.7 us -> 94.7 us  [the longest x22 68.6 us: hop_up(): return lax.ppermute(x, 'col', [(c, c + 1) for c in range(first, last)])]
    convert_element_type x4 -> x0, local copies, waits for them, and re-layouts: 9.3 us -> none  [sum_along(): send_up.astype(jnp.bfloat16)]
    convert_element_type x12 -> x10, other arithmetic: 4.86 us -> 10.9 us  [the longest x5 7.37 us: step_sum(): (share[step + 1] + down.astype(jnp.float32)).astype(jnp.bfloat16)]
  transfers between devices with their start and end apart: 46 -> 59, of which waited for: 14 -> 11; matrix products, arithmetic and copies ran while one was open for 5% -> 13% of each run, Pallas kernels for 52% -> 18%
where the time goes in v2:
time: 306 us; the launch traced here: 300 us
  starting transfers between devices  102 us (33%)
  waiting for transfers between devices  86.7 us (28%)
  Pallas kernels  58.4 us (19%)
  local copies, waits for them, and re-layouts  29.6 us (10%)
  other arithmetic  21.8 us (7%)
    ppermute x22, starting transfers between devices, hop_up(): return lax.ppermute(x, 'col', [(c, c + 1) for c in range(first, last)])  68.6 us
    ppermute x22, waiting for transfers between devices, hop_down(): lax.ppermute(x, 'col', [(cols - 1 - c, cols - 2 - c) for c in range(first...  59.9 us
    pallas_call x4, Pallas kernels, run_chunk(): pl.pallas_call(functools.partial(chunk_kernel, pieces, cols, steps, chunk...  55.1 us
    ppermute x22, waiting for transfers between devices, hop_up(): return lax.ppermute(x, 'col', [(c, c + 1) for c in range(first, last)])  26.8 us
    ppermute x22, starting transfers between devices, hop_down(): lax.ppermute(x, 'col', [(cols - 1 - c, cols - 2 - c) for c in range(first...  26.2 us
    unnamed x68, local copies, waits for them, and re-layouts  11.8 us
    convert_element_type x5, other arithmetic, step_sum(): (share[step + 1] + down.astype(jnp.float32)).astype(jnp.bfloat16)  7.37 us
  transfers between devices with their start and end apart: 59, of which 11 were waited for; matrix products, arithmetic and copies ran while one was open for 13% of the time, Pallas kernels for 18%

profile of v2, /device:TPU:0, one launch (start us, length us, event | category | flops | bytes accessed | tf_op | source)
XLA Modules:
  0.0 300.4 jit_solution(2541046841420617875)
XLA Ops:
  0.6 3.7 %copy.19 = bf16[384,2,1024]{0,2,1:T(8,128)(2,1)S(1)} copy(bf16[384,2,1024]{2,1,0:T(2,128)(2,1)} %param.4) | data formatting | bytes 3145728 | tf_op args[0]
  7.1 1.8 copy.30
  8.9 2.6 collective-permute-start
  11.5 1.5 collective-permute-start.1
  13.0 1.5 copy.20
  14.6 3.5 %collective-permute-start.11 = (bf16[1,2,2,384,128]{4,3,2,1,0:T(8,128)(2,1)S(1)}, bf16[1,2,2,384,128]{4,3,2,1,0:T(8,128)(2,1)S(1)}, u32[]{:S(2)}, u32[]{:S(2)}) collective-permute-start(bf16[1,2,2,384,128]{4,3,2,1,0:T(8,128)(2,1)S(1)} %fusion.21), channel_id=1, source_target_pairs={{0,1},{1,2},{2,3},{4,5},{5,6},{6,7},{8,9},{9,10},{10,11},{12,13},{... | collective-permute-start | bytes 1179656 | tf_op jit(solution)/shard_map/ppermute | solution.py:273
  18.2 1.3 collective-permute-start.14
  19.5 7.1 %collective-permute-done.11.refs_11_ = bf16[1,2,2,384,128]{4,3,2,1,0:T(8,128)(2,1)S(1)} collective-permute-done((bf16[1,2,2,384,128]{4,3,2,1,0:T(8,128)(2,1)S(1)}, bf16[1,2,2,384,128]{4,3,2,1,0:T(8,128)(2,1)S(1)}, u32[]{:S(2)}, u32[]{:S(2)}) %collective-permute-start.11) | collective-permute-done | bytes 393248 | tf_op jit(solution)/shard_map/ppermute | solution.py:273
  27.4 4.2 %collective-permute-done.14.refs_14_ = bf16[1,2,2,384,128]{4,3,2,1,0:T(8,128)(2,1)S(1)} collective-permute-done((bf16[1,2,2,384,128]{4,3,2,1,0:T(8,128)(2,1)S(1)}, bf16[1,2,2,384,128]{4,3,2,1,0:T(8,128)(2,1)S(1)}, u32[]{:S(2)}, u32[]{:S(2)}) %collective-permute-start.14) | collective-permute-done | bytes 393248 | tf_op jit(solution)/shard_map/ppermute | solution.py:278
  31.6 3.5 %collective-permute-start.10 = (bf16[3,2,2,384,128]{4,3,2,1,0:T(8,128)(2,1)S(1)}, bf16[3,2,2,384,128]{4,3,2,1,0:T(8,128)(2,1)S(1)}, u32[]{:S(2)}, u32[]{:S(2)}) collective-permute-start(bf16[3,2,2,384,128]{4,3,2,1,0:T(8,128)(2,1)S(1)} %fusion), channel_id=1, source_target_pairs={{0,1},{1,2},{2,3},{4,5},{5,6},{6,7},{8,9},{9,10},{10,11},{12,13},{... | collective-permute-start | bytes 3538952 | tf_op jit(solution)/shard_map/ppermute | solution.py:273
  35.1 1.3 collective-permute-start.15
  36.4 13.3 %collective-permute-done.15.refs_15_ = bf16[1,2,2,384,128]{4,3,2,1,0:T(8,128)(2,1)S(1)} collective-permute-done((bf16[1,2,2,384,128]{4,3,2,1,0:T(8,128)(2,1)S(1)}, bf16[1,2,2,384,128]{4,3,2,1,0:T(8,128)(2,1)S(1)}, u32[]{:S(2)}, u32[]{:S(2)}) %collective-permute-start.15) | collective-permute-done | bytes 393248 | tf_op jit(solution)/shard_map/ppermute | solution.py:278
  49.7 1.3 collective-permute-start.25
  51.7 1.3 collective-permute-start.16
  54.8 1.2 slice.175
  57.3 26.7 %collective-permute-done.16.refs_16_ = bf16[1,2,2,384,128]{4,3,2,1,0:T(8,128)(2,1)S(1)} collective-permute-done((bf16[1,2,2,384,128]{4,3,2,1,0:T(8,128)(2,1)S(1)}, bf16[1,2,2,384,128]{4,3,2,1,0:T(8,128)(2,1)S(1)}, u32[]{:S(2)}, u32[]{:S(2)}) %collective-permute-start.16) | collective-permute-done | bytes 393248 | tf_op jit(solution)/shard_map/ppermute | solution.py:278
  89.1 1.3 collective-permute-start.26
  93.4 2.8 pad_maximum_fusion.refs_10_
  96.3 10.5 %collective-permute-done.26.refs_15_ = bf16[1,2,2,384,128]{4,3,2,1,0:T(8,128)(2,1)} collective-permute-done((bf16[1,2,2,384,128]{4,3,2,1,0:T(8,128)(2,1)}, bf16[1,2,2,384,128]{4,3,2,1,0:T(8,128)(2,1)}, u32[]{:S(2)}, u32[]{:S(2)}) %collective-permute-start.26) | collective-permute-done | bytes 393248 | tf_op jit(solution)/shard_map/ppermute | solution.py:278
  107.5 1.3 collective-permute-start.38
  109.5 1.3 collective-permute-start.27
  110.9 14.2 %shard_map.59 = (bf16[2,2,1024,1024]{3,2,1,0:T(8,128)(2,1)}, bf16[2,2,512,1024]{3,2,1,0:T(8,128)(2,1)}, f32[4,768,256]{2,1,0:T(8,128)}, bf16[768,256]{1,0:T(8,128)(2,1)S(1)}, bf16[768,256]{1,0:T(8,128)(2,1)S(1)}) custom-call(bf16[384,2048]{1,0:T(8,128)(2,1)} %bitcast.114, bf16[384,2048]{1,0:T(8,128)(2,1)} %collective-permute-done.refs_1_, ...), custom_call_target="tpu_custom_call" | custom-call | flops 6442450944 | bytes 12582912 | tf_op jit(solution)/shard_map/pallas_call | solution.py:191
  125.2 5.2 %collective-permute-start.17 = (bf16[768,256]{1,0:T(8,128)(2,1)S(1)}, bf16[768,256]{1,0:T(8,128)(2,1)S(1)}, u32[]{:S(2)}, u32[]{:S(2)}) collective-permute-start(bf16[768,256]{1,0:T(8,128)(2,1)S(1)} %get-tuple-element.31), channel_id=1, source_target_pairs={{0,1},{4,5},{8,9},{12,13},{16,17},{20,21},{24,25},{28,29}} | collective-permute-start | bytes 1179656 | tf_op jit(solution)/shard_map/ppermute | solution.py:273
  131.1 12.9 %shard_map.60 = (bf16[2,2,1024,1024]{3,2,1,0:T(8,128)(2,1)}, bf16[2,2,512,1024]{3,2,1,0:T(8,128)(2,1)}, f32[4,768,256]{2,1,0:T(8,128)}, bf16[768,256]{1,0:T(8,128)(2,1)}, bf16[768,256]{1,0:T(8,128)(2,1)}) custom-call(bf16[384,2048]{1,0:T(8,128)(2,1)} %bitcast.115, ...), custom_call_target="tpu_custom_call", output_to_operand_aliasing={{0}: (20, {}), {1}: (21, {})} | custom-call | flops 6442450944 | bytes 12582912 | tf_op jit(solution)/shard_map/pallas_call | solution.py:191
  144.0 2.1 collective-permute-start.28
  146.1 1.4 collective-permute-start.30
  147.5 2.1 fusion.19
  149.7 2.1 collective-permute-start.18
  152.5 1.4 collective-permute-start.20
  156.1 1.3 collective-permute-start.39
  157.4 2.4 fusion.16
  159.8 1.4 collective-permute-done.18
  161.1 1.3 collective-permute-start.34
  162.4 7.1 %collective-permute-start.29 = (bf16[768,256]{1,0:T(8,128)(2,1)}, bf16[768,256]{1,0:T(8,128)(2,1)}, u32[]{:S(2)}, u32[]{:S(2)}) collective-permute-start(bf16[768,256]{1,0:T(8,128)(2,1)} %get-tuple-element.65), channel_id=1, source_target_pairs={{0,1},{1,2},{4,5},{5,6},{8,9},{9,10},{12,13},{13,14},{16,17},{17,1... | collective-permute-start | bytes 1179656 | tf_op jit(solution)/shard_map/ppermute | solution.py:273
  169.5 2.6 fusion.17
  173.0 1.5 collective-permute-start.31
  174.4 3.8 %collective-permute-start.21 = (bf16[768,256]{1,0:T(8,128)(2,1)}, bf16[768,256]{1,0:T(8,128)(2,1)}, u32[]{:S(2)}, u32[]{:S(2)}) collective-permute-start(bf16[768,256]{1,0:T(8,128)(2,1)} %get-tuple-element.67), channel_id=1, source_target_pairs={{0,1},{1,2},{2,3},{4,5},{5,6},{6,7},{8,9},{9,10},{10,11},{12,13},{... | collective-permute-start | bytes 1179656 | tf_op jit(solution)/shard_map/ppermute | solution.py:273
  178.2 1.3 collective-permute-start.22
  179.5 14.0 %shard_map.61 = (bf16[2,2,1024,1024]{3,2,1,0:T(8,128)(2,1)}, bf16[2,2,512,1024]{3,2,1,0:T(8,128)(2,1)}, f32[4,768,256]{2,1,0:T(8,128)}, bf16[768,256]{1,0:T(8,128)(2,1)}, bf16[768,256]{1,0:T(8,128)(2,1)S(1)}) custom-call(bf16[384,2048]{1,0:T(8,128)(2,1)} %bitcast.116, ...), custom_call_target="tpu_custom_call", output_to_operand_aliasing={{0}: (20, {}), {1}: (21, {})} | custom-call | flops 6442450944 | bytes 12582912 | tf_op jit(solution)/shard_map/pallas_call | solution.py:191
  195.1 5.3 %collective-permute-start.43 = (bf16[768,256]{1,0:T(8,128)(2,1)}, bf16[768,256]{1,0:T(8,128)(2,1)}, u32[]{:S(2)}, u32[]{:S(2)}) collective-permute-start(bf16[768,256]{1,0:T(8,128)(2,1)} %get-tuple-element.53), channel_id=1, source_target_pairs={{0,1},{4,5},{8,9},{12,13},{16,17},{20,21},{24,25},{28,29}} | collective-permute-start | bytes 1179656 | tf_op jit(solution)/shard_map/ppermute | solution.py:273
  201.1 1.3 collective-permute-start.35
  203.3 1.9 fusion.12
  205.2 4.7 %collective-permute-start.41 = (bf16[768,256]{1,0:T(8,128)(2,1)S(1)}, bf16[768,256]{1,0:T(8,128)(2,1)S(1)}, u32[]{:S(2)}, u32[]{:S(2)}) collective-permute-start(bf16[768,256]{1,0:T(8,128)(2,1)S(1)} %get-tuple-element.58), channel_id=1, source_target_pairs={{0,1},{1,2},{2,3},{4,5},{5,6},{6,7},{8,9},{9,10},{10,11},{12,13},{... | collective-permute-start | bytes 1179656 | tf_op jit(solution)/shard_map/ppermute | solution.py:273
  209.9 1.3 collective-permute-start.42
  212.3 4.6 %collective-permute-start.44 = (bf16[768,256]{1,0:T(8,128)(2,1)S(1)}, bf16[768,256]{1,0:T(8,128)(2,1)S(1)}, u32[]{:S(2)}, u32[]{:S(2)}) collective-permute-start(bf16[768,256]{1,0:T(8,128)(2,1)S(1)} %fusion.7), channel_id=1, source_target_pairs={{0,1},{1,2},{4,5},{5,6},{8,9},{9,10},{12,13},{13,14},{16,17},{17,1... | collective-permute-start | bytes 1179656 | tf_op jit(solution)/shard_map/ppermute | solution.py:273
  216.9 13.9 %shard_map.62 = (bf16[2,2,1024,1024]{3,2,1,0:T(8,128)(2,1)}, bf16[2,2,512,1024]{3,2,1,0:T(8,128)(2,1)}, f32[4,768,256]{2,1,0:T(8,128)}, bf16[768,256]{1,0:T(8,128)(2,1)S(1)}, bf16[768,256]{1,0:T(8,128)(2,1)S(1)}) custom-call(bf16[384,2048]{1,0:T(8,128)(2,1)} %bitcast.117, ...), custom_call_target="tpu_custom_call", output_to_operand_aliasing={{0}: (20, {}), {1}: (21, {})} | custom-call | flops 6442450944 | bytes 12582912 | tf_op jit(solution)/shard_map/pallas_call | solution.py:191
  230.9 3.4 %collective-permute-start.49 = (bf16[768,256]{1,0:T(8,128)(2,1)S(1)}, bf16[768,256]{1,0:T(8,128)(2,1)S(1)}, u32[]{:S(2)}, u32[]{:S(2)}) collective-permute-start(bf16[768,256]{1,0:T(8,128)(2,1)S(1)} %get-tuple-element.56), channel_id=1, source_target_pairs={{0,1},{4,5},{8,9},{12,13},{16,17},{20,21},{24,25},{28,29}} | collective-permute-start | bytes 1179656 | tf_op jit(solution)/shard_map/ppermute | solution.py:273
  234.3 1.5 fusion.14
  236.6 3.0 collective-permute-done.49
  240.4 4.4 %collective-permute-start.50 = (bf16[768,256]{1,0:T(8,128)(2,1)S(1)}, bf16[768,256]{1,0:T(8,128)(2,1)S(1)}, u32[]{:S(2)}, u32[]{:S(2)}) collective-permute-start(bf16[768,256]{1,0:T(8,128)(2,1)S(1)} %fusion.2), channel_id=1, source_target_pairs={{0,1},{1,2},{4,5},{5,6},{8,9},{9,10},{12,13},{13,14},{16,17},{17,1... | collective-permute-start | bytes 1179656 | tf_op jit(solution)/shard_map/ppermute | solution.py:273
  246.0 1.2 fusion.13
  247.3 2.8 collective-permute-start.45
  250.1 4.2 %collective-permute-done.50 = bf16[768,256]{1,0:T(8,128)(2,1)S(1)} collective-permute-done((bf16[768,256]{1,0:T(8,128)(2,1)S(1)}, bf16[768,256]{1,0:T(8,128)(2,1)S(1)}, u32[]{:S(2)}, u32[]{:S(2)}) %collective-permute-start.50) | collective-permute-done | bytes 393248 | tf_op jit(solution)/shard_map/ppermute | solution.py:273
  255.3 1.3 collective-permute-start.48
  257.5 4.7 %collective-permute-done.45 = bf16[768,256]{1,0:T(8,128)(2,1)S(1)} collective-permute-done((bf16[768,256]{1,0:T(8,128)(2,1)S(1)}, bf16[768,256]{1,0:T(8,128)(2,1)S(1)}, u32[]{:S(2)}, u32[]{:S(2)}) %collective-permute-start.45) | collective-permute-done | bytes 393248 | tf_op jit(solution)/shard_map/ppermute | solution.py:273
  262.2 10.7 %collective-permute-start.51 = (bf16[768,256]{1,0:T(8,128)(2,1)S(1)}, bf16[768,256]{1,0:T(8,128)(2,1)S(1)}, u32[]{:S(2)}, u32[]{:S(2)}) collective-permute-start(bf16[768,256]{1,0:T(8,128)(2,1)S(1)} %get-tuple-element.62), channel_id=1, source_target_pairs={{0,1},{1,2},{2,3},{4,5},{5,6},{6,7},{8,9},{9,10},{10,11},{12,13},{... | collective-permute-start | bytes 1179656 | tf_op jit(solution)/shard_map/ppermute | solution.py:273
  273.0 1.6 collective-permute-start.54
  275.5 6.5 %collective-permute-done.51 = bf16[768,256]{1,0:T(8,128)(2,1)S(1)} collective-permute-done((bf16[768,256]{1,0:T(8,128)(2,1)S(1)}, bf16[768,256]{1,0:T(8,128)(2,1)S(1)}, u32[]{:S(2)}, u32[]{:S(2)}) %collective-permute-start.51) | collective-permute-done | bytes 393248 | tf_op jit(solution)/shard_map/ppermute | solution.py:273
  282.0 5.1 %collective-permute-done.54 = bf16[768,256]{1,0:T(8,128)(2,1)S(1)} collective-permute-done((bf16[768,256]{1,0:T(8,128)(2,1)S(1)}, bf16[768,256]{1,0:T(8,128)(2,1)S(1)}, u32[]{:S(2)}, u32[]{:S(2)}) %collective-permute-start.54) | collective-permute-done | bytes 393248 | tf_op jit(solution)/shard_map/ppermute | solution.py:278
  289.3 1.2 stack.49
  290.5 1.2 stack.50
  291.7 1.5 copy_bitcast_fusion
  293.2 3.6 %maximum_select_fusion = f32[384,2,1024]{2,1,0:T(2,128)} fusion(f32[384,2,512]{2,1,0:T(2,128)S(1)} %get-tuple-element.90, f32[384,2,512]{2,1,0:T(2,128)S(1)} %get-tuple-element.91, pred[]{:T(512)S(6)} %eq.3), kind=kLoop, calls=%fused_computation | loop fusion | flops 2359296 | bytes 6291457 | tf_op jit(solution)/shard_map/jit(_where)/select_n | solution.py:381
  296.8 3.3 %shard_map.63 = bf16[2,2,1024,1024]{3,2,1,0:T(8,128)(2,1)} custom-call(bf16[2,2,512,1024]{3,2,1,0:T(8,128)(2,1)} %collective-permute-done.40.other, bf16[2,2,1024,1024]{3,2,1,0:T(8,128)(2,1)} %get-tuple-element.47._), custom_call_target="tpu_custom_call", output_to_operand_aliasing={{}: (1, {})} | custom-call | bytes 8388608 | tf_op jit(solution)/shard_map/pallas_call | solution.py:246
  (172 shorter events, 33.2 us)
Async XLA Ops:
  6.6 7.9 %collective-permute-start.9 = (bf16[4,2,384,128]{3,2,1,0:T(8,128)(2,1)}, bf16[4,2,384,128]{3,2,1,0:T(8,128)(2,1)S(1)}, u32[]{:S(2)}, u32[]{:S(2)}) collective-permute-start(bf16[4,2,384,128]{3,2,1,0:T(8,128)(2,1)} %bitcast.5), channel_id=1, source_target_pairs={{0,16},{16,0},{1,17},{17,1},{2,18},{18,2},{3,19},{19,3},{4,20},{20... | collective-permute-start | bytes 2359304 | tf_op jit(solution)/shard_map/ppermute | solution.py:264
  8.9 42.1 %collective-permute-start = (bf16[384,2048]{1,0:T(8,128)(2,1)S(1)}, bf16[384,2048]{1,0:T(8,128)(2,1)}, u32[]{:S(2)}, u32[]{:S(2)}) collective-permute-start(bf16[384,2048]{1,0:T(8,128)(2,1)S(1)} %bitcast.111), channel_id=1, source_target_pairs={{0,4},{4,0},{8,12},{12,8},{1,5},{5,1},{9,13},{13,9},{2,6},{6,2},{1... | collective-permute-start | bytes 4718600 | tf_op jit(solution)/shard_map/ppermute | solution.py:268
  11.5 40.2 %collective-permute-start.1 = (bf16[384,2048]{1,0:T(8,128)(2,1)S(1)}, bf16[384,2048]{1,0:T(8,128)(2,1)}, u32[]{:S(2)}, u32[]{:S(2)}) collective-permute-start(bf16[384,2048]{1,0:T(8,128)(2,1)S(1)} %bitcast.112), channel_id=1, source_target_pairs={{0,8},{4,12},{8,0},{12,4},{1,9},{5,13},{9,1},{13,5},{2,10},{6,14},... | collective-permute-start | bytes 4718600 | tf_op jit(solution)/shard_map/ppermute | solution.py:268
  14.6 12.0 %collective-permute-start.11 = (bf16[1,2,2,384,128]{4,3,2,1,0:T(8,128)(2,1)S(1)}, bf16[1,2,2,384,128]{4,3,2,1,0:T(8,128)(2,1)S(1)}, u32[]{:S(2)}, u32[]{:S(2)}) collective-permute-start(bf16[1,2,2,384,128]{4,3,2,1,0:T(8,128)(2,1)S(1)} %fusion.21), channel_id=1, source_target_pairs={{0,1},{1,2},{2,3},{4,5},{5,6},{6,7},{8,9},{9,10},{10,11},{12,13},{... | collective-permute-start | bytes 1179656 | tf_op jit(solution)/shard_map/ppermute | solution.py:273
  18.1 36.1 %collective-permute-start.4 = (bf16[384,2048]{1,0:T(8,128)(2,1)S(1)}, bf16[384,2048]{1,0:T(8,128)(2,1)S(1)}, u32[]{:S(2)}, u32[]{:S(2)}) collective-permute-start(bf16[384,2048]{1,0:T(8,128)(2,1)S(1)} %bitcast.113), channel_id=1, source_target_pairs={{0,16},{16,0},{1,17},{17,1},{2,18},{18,2},{3,19},{19,3},{4,20},{20... | collective-permute-start | bytes 4718600 | tf_op jit(solution)/shard_map/ppermute | solution.py:264
  18.2 13.4 %collective-permute-start.14 = (bf16[1,2,2,384,128]{4,3,2,1,0:T(8,128)(2,1)S(1)}, bf16[1,2,2,384,128]{4,3,2,1,0:T(8,128)(2,1)S(1)}, u32[]{:S(2)}, u32[]{:S(2)}) collective-permute-start(bf16[1,2,2,384,128]{4,3,2,1,0:T(8,128)(2,1)S(1)} %fusion.21), channel_id=1, source_target_pairs={{3,2},{2,1},{1,0},{7,6},{6,5},{5,4},{11,10},{10,9},{9,8},{15,14},{... | collective-permute-start | bytes 1179656 | tf_op jit(solution)/shard_map/ppermute | solution.py:278
  26.5 27.7 %copy-start.14 = (bf16[1,2,2,384,128]{4,3,2,1,0:T(8,128)(2,1)}, bf16[1,2,2,384,128]{4,3,2,1,0:T(8,128)(2,1)S(1)}, u32[]{:S(2)}) copy-start(bf16[1,2,2,384,128]{4,3,2,1,0:T(8,128)(2,1)S(1)} %collective-permute-done.11.refs_11_) | copy-start | bytes 1179652
  26.5 8.6 %collective-permute-start.12 = (bf16[1,2,2,384,128]{4,3,2,1,0:T(8,128)(2,1)S(1)}, bf16[1,2,2,384,128]{4,3,2,1,0:T(8,128)(2,1)S(1)}, u32[]{:S(2)}, u32[]{:S(2)}) collective-permute-start(bf16[1,2,2,384,128]{4,3,2,1,0:T(8,128)(2,1)S(1)} %collective-permute-done.11.refs_11_), channel_id=1, source_target_pairs={{1,2},{2,3},{5,6},{6,7},{9,10},{10,11},{13,14},{14,15},{17,18},{18... | collective-permute-start | bytes 1179656 | tf_op jit(solution)/shard_map/ppermute | solution.py:273
  31.6 24.4 %copy-start.16 = (bf16[1,2,2,384,128]{4,3,2,1,0:T(8,128)(2,1)}, bf16[1,2,2,384,128]{4,3,2,1,0:T(8,128)(2,1)S(1)}, u32[]{:S(2)}) copy-start(bf16[1,2,2,384,128]{4,3,2,1,0:T(8,128)(2,1)S(1)} %collective-permute-done.14.refs_14_) | copy-start | bytes 1179652
  31.6 53.3 %collective-permute-start.10 = (bf16[3,2,2,384,128]{4,3,2,1,0:T(8,128)(2,1)S(1)}, bf16[3,2,2,384,128]{4,3,2,1,0:T(8,128)(2,1)S(1)}, u32[]{:S(2)}, u32[]{:S(2)}) collective-permute-start(bf16[3,2,2,384,128]{4,3,2,1,0:T(8,128)(2,1)S(1)} %fusion), channel_id=1, source_target_pairs={{0,1},{1,2},{2,3},{4,5},{5,6},{6,7},{8,9},{9,10},{10,11},{12,13},{... | collective-permute-start | bytes 3538952 | tf_op jit(solution)/shard_map/ppermute | solution.py:273
  35.1 20.9 %copy-start.18 = (bf16[1,2,2,384,128]{4,3,2,1,0:T(8,128)(2,1)}, bf16[1,2,2,384,128]{4,3,2,1,0:T(8,128)(2,1)S(1)}, u32[]{:S(2)}) copy-start(bf16[1,2,2,384,128]{4,3,2,1,0:T(8,128)(2,1)S(1)} %collective-permute-done.12.refs_12_) | copy-start | bytes 1179652
  35.1 14.6 %collective-permute-start.15 = (bf16[1,2,2,384,128]{4,3,2,1,0:T(8,128)(2,1)S(1)}, bf16[1,2,2,384,128]{4,3,2,1,0:T(8,128)(2,1)S(1)}, u32[]{:S(2)}, u32[]{:S(2)}) collective-permute-start(bf16[1,2,2,384,128]{4,3,2,1,0:T(8,128)(2,1)S(1)} %collective-permute-done.14.refs_14_), channel_id=1, source_target_pairs={{2,1},{1,0},{6,5},{5,4},{10,9},{9,8},{14,13},{13,12},{18,17},{17,1... | collective-permute-start | bytes 1179656 | tf_op jit(solution)/shard_map/ppermute | solution.py:278
  49.7 35.8 %collective-permute-start.25 = (bf16[3,2,2,384,128]{4,3,2,1,0:T(8,128)(2,1)S(1)}, bf16[3,2,2,384,128]{4,3,2,1,0:T(8,128)(2,1)S(1)}, u32[]{:S(2)}, u32[]{:S(2)}) collective-permute-start(bf16[3,2,2,384,128]{4,3,2,1,0:T(8,128)(2,1)S(1)} %fusion), channel_id=1, source_target_pairs={{3,2},{2,1},{1,0},{7,6},{6,5},{5,4},{11,10},{10,9},{9,8},{15,14},{... | collective-permute-start | bytes 3538952 | tf_op jit(solution)/shard_map/ppermute | solution.py:278
  51.0 5.0 %collective-permute-start.13 = (bf16[1,2,2,384,128]{4,3,2,1,0:T(8,128)(2,1)S(1)}, bf16[1,2,2,384,128]{4,3,2,1,0:T(8,128)(2,1)S(1)}, u32[]{:S(2)}, u32[]{:S(2)}) collective-permute-start(bf16[1,2,2,384,128]{4,3,2,1,0:T(8,128)(2,1)S(1)} %collective-permute-done.12.refs_12_), channel_id=1, source_target_pairs={{2,3},{6,7},{10,11},{14,15},{18,19},{22,23},{26,27},{30,31}} | collective-permute-start | bytes 1179656 | tf_op jit(solution)/shard_map/ppermute | solution.py:273
  51.7 32.4 %collective-permute-start.16 = (bf16[1,2,2,384,128]{4,3,2,1,0:T(8,128)(2,1)S(1)}, bf16[1,2,2,384,128]{4,3,2,1,0:T(8,128)(2,1)S(1)}, u32[]{:S(2)}, u32[]{:S(2)}) collective-permute-start(bf16[1,2,2,384,128]{4,3,2,1,0:T(8,128)(2,1)S(1)} %collective-permute-done.15.refs_15_), channel_id=1, source_target_pairs={{1,0},{5,4},{9,8},{13,12},{17,16},{21,20},{25,24},{29,28}} | collective-permute-start | bytes 1179656 | tf_op jit(solution)/shard_map/ppermute | solution.py:278
  54.2 31.2 %copy-start.28 = (bf16[384,2048]{1,0:T(8,128)(2,1)}, bf16[384,2048]{1,0:T(8,128)(2,1)S(1)}, u32[]{:S(2)}) copy-start(bf16[384,2048]{1,0:T(8,128)(2,1)S(1)} %collective-permute-done.4.refs_5_) | copy-start | bytes 4718596
  54.2 32.7 %collective-permute-start.2 = (bf16[192,2048]{1,0:T(8,128)(2,1)S(1)}, bf16[192,2048]{1,0:T(8,128)(2,1)S(1)}, u32[]{:S(2)}, u32[]{:S(2)}) collective-permute-start(bf16[192,2048]{1,0:T(8,128)(2,1)S(1)} %slice.174), channel_id=1, source_target_pairs={{0,8},{4,12},{8,0},{12,4},{1,9},{5,13},{9,1},{13,5},{2,10},{6,14},... | collective-permute-start | bytes 2359304 | tf_op jit(solution)/shard_map/ppermute | solution.py:268
  56.8 30.1 %collective-permute-start.3 = (bf16[192,2048]{1,0:T(8,128)(2,1)S(1)}, bf16[192,2048]{1,0:T(8,128)(2,1)S(1)}, u32[]{:S(2)}, u32[]{:S(2)}) collective-permute-start(bf16[192,2048]{1,0:T(8,128)(2,1)S(1)} %slice.175), channel_id=1, source_target_pairs={{0,4},{4,0},{8,12},{12,8},{1,5},{5,1},{9,13},{13,9},{2,6},{6,2},{1... | collective-permute-start | bytes 2359304 | tf_op jit(solution)/shard_map/ppermute | solution.py:268
  84.8 24.7 %collective-permute-start.5 = (bf16[384,2048]{1,0:T(8,128)(2,1)}, bf16[384,2048]{1,0:T(8,128)(2,1)}, u32[]{:S(2)}, u32[]{:S(2)}) collective-permute-start(bf16[384,2048]{1,0:T(8,128)(2,1)} %collective-permute-done.refs_1_), channel_id=1, source_target_pairs={{0,16},{16,0},{1,17},{17,1},{2,18},{18,2},{3,19},{19,3},{4,20},{20... | collective-permute-start | bytes 4718600 | tf_op jit(solution)/shard_map/ppermute | solution.py:264
  84.8 26.0 %collective-permute-start.6 = (bf16[384,2048]{1,0:T(8,128)(2,1)}, bf16[384,2048]{1,0:T(8,128)(2,1)}, u32[]{:S(2)}, u32[]{:S(2)}) collective-permute-start(bf16[384,2048]{1,0:T(8,128)(2,1)} %collective-permute-done.1.refs_2_), channel_id=1, source_target_pairs={{0,16},{16,0},{1,17},{17,1},{2,18},{18,2},{3,19},{19,3},{4,20},{20... | collective-permute-start | bytes 4718600 | tf_op jit(solution)/shard_map/ppermute | solution.py:264
  85.5 2.9 collective-permute-start.23
  86.9 20.6 %collective-permute-start.7 = (bf16[192,2048]{1,0:T(8,128)(2,1)S(1)}, bf16[192,2048]{1,0:T(8,128)(2,1)S(1)}, u32[]{:S(2)}, u32[]{:S(2)}) collective-permute-start(bf16[192,2048]{1,0:T(8,128)(2,1)S(1)} %collective-permute-done.2.refs_3_), channel_id=1, source_target_pairs={{0,16},{16,0},{1,17},{17,1},{2,18},{18,2},{3,19},{19,3},{4,20},{20... | collective-permute-start | bytes 2359304 | tf_op jit(solution)/shard_map/ppermute | solution.py:264
  86.9 21.9 %collective-permute-start.8 = (bf16[192,2048]{1,0:T(8,128)(2,1)S(1)}, bf16[192,2048]{1,0:T(8,128)(2,1)}, u32[]{:S(2)}, u32[]{:S(2)}) collective-permute-start(bf16[192,2048]{1,0:T(8,128)(2,1)S(1)} %collective-permute-done.3.refs_4_), channel_id=1, source_target_pairs={{0,16},{16,0},{1,17},{17,1},{2,18},{18,2},{3,19},{19,3},{4,20},{20... | collective-permute-start | bytes 2359304 | tf_op jit(solution)/shard_map/ppermute | solution.py:264
  89.1 17.7 %collective-permute-start.26 = (bf16[1,2,2,384,128]{4,3,2,1,0:T(8,128)(2,1)}, bf16[1,2,2,384,128]{4,3,2,1,0:T(8,128)(2,1)}, u32[]{:S(2)}, u32[]{:S(2)}) collective-permute-start(bf16[1,2,2,384,128]{4,3,2,1,0:T(8,128)(2,1)} %get-tuple-element.74.refs_14_), channel_id=1, source_target_pairs={{2,1},{1,0},{6,5},{5,4},{10,9},{9,8},{14,13},{13,12},{18,17},{17,1... | collective-permute-start | bytes 1179656 | tf_op jit(solution)/shard_map/ppermute | solution.py:278
  106.8 44.9 %collective-permute-start.36 = (bf16[1,2,2,384,128]{4,3,2,1,0:T(8,128)(2,1)S(1)}, bf16[1,2,2,384,128]{4,3,2,1,0:T(8,128)(2,1)S(1)}, u32[]{:S(2)}, u32[]{:S(2)}) collective-permute-start(bf16[1,2,2,384,128]{4,3,2,1,0:T(8,128)(2,1)S(1)} %get-tuple-element.41.refs_11_), channel_id=1, source_target_pairs={{1,2},{2,3},{5,6},{6,7},{9,10},{10,11},{13,14},{14,15},{17,18},{18... | collective-permute-start | bytes 1179656 | tf_op jit(solution)/shard_map/ppermute | solution.py:273
  107.5 47.2 %collective-permute-start.38 = (bf16[1,2,2,384,128]{4,3,2,1,0:T(8,128)(2,1)}, bf16[1,2,2,384,128]{4,3,2,1,0:T(8,128)(2,1)}, u32[]{:S(2)}, u32[]{:S(2)}) collective-permute-start(bf16[1,2,2,384,128]{4,3,2,1,0:T(8,128)(2,1)} %get-tuple-element.72.refs_14_), channel_id=1, source_target_pairs={{2,1},{1,0},{6,5},{5,4},{10,9},{9,8},{14,13},{13,12},{18,17},{17,1... | collective-permute-start | bytes 1179656 | tf_op jit(solution)/shard_map/ppermute | solution.py:278
  108.8 21.6 %collective-permute-start.24 = (bf16[1,2,2,384,128]{4,3,2,1,0:T(8,128)(2,1)S(1)}, bf16[1,2,2,384,128]{4,3,2,1,0:T(8,128)(2,1)S(1)}, u32[]{:S(2)}, u32[]{:S(2)}) collective-permute-start(bf16[1,2,2,384,128]{4,3,2,1,0:T(8,128)(2,1)S(1)} %copy-done.7), channel_id=1, source_target_pairs={{2,3},{6,7},{10,11},{14,15},{18,19},{22,23},{26,27},{30,31}} | collective-permute-start | bytes 1179656 | tf_op jit(solution)/shard_map/ppermute | solution.py:273
  109.5 21.6 %collective-permute-start.27 = (bf16[1,2,2,384,128]{4,3,2,1,0:T(8,128)(2,1)}, bf16[1,2,2,384,128]{4,3,2,1,0:T(8,128)(2,1)S(1)}, u32[]{:S(2)}, u32[]{:S(2)}) collective-permute-start(bf16[1,2,2,384,128]{4,3,2,1,0:T(8,128)(2,1)} %collective-permute-done.26.refs_15_), channel_id=1, source_target_pairs={{1,0},{5,4},{9,8},{13,12},{17,16},{21,20},{25,24},{29,28}} | collective-permute-start | bytes 1179656 | tf_op jit(solution)/shard_map/ppermute | solution.py:278
  110.9 20.2 %copy-start.1 = (bf16[1,2,2,384,128]{4,3,2,1,0:T(8,128)(2,1)S(1)}, bf16[1,2,2,384,128]{4,3,2,1,0:T(8,128)(2,1)}, u32[]{:S(2)}) copy-start(bf16[1,2,2,384,128]{4,3,2,1,0:T(8,128)(2,1)} %copy-done) | copy-start | bytes 1179652
  125.2 20.9 %collective-permute-start.17 = (bf16[768,256]{1,0:T(8,128)(2,1)S(1)}, bf16[768,256]{1,0:T(8,128)(2,1)S(1)}, u32[]{:S(2)}, u32[]{:S(2)}) collective-permute-start(bf16[768,256]{1,0:T(8,128)(2,1)S(1)} %get-tuple-element.31), channel_id=1, source_target_pairs={{0,1},{4,5},{8,9},{12,13},{16,17},{20,21},{24,25},{28,29}} | collective-permute-start | bytes 1179656 | tf_op jit(solution)/shard_map/ppermute | solution.py:273
  130.4 17.1 %collective-permute-start.19 = (bf16[768,256]{1,0:T(8,128)(2,1)S(1)}, bf16[768,256]{1,0:T(8,128)(2,1)S(1)}, u32[]{:S(2)}, u32[]{:S(2)}) collective-permute-start(bf16[768,256]{1,0:T(8,128)(2,1)S(1)} %get-tuple-element.32), channel_id=1, source_target_pairs={{3,2},{7,6},{11,10},{15,14},{19,18},{23,22},{27,26},{31,30}} | collective-permute-start | bytes 1179656 | tf_op jit(solution)/shard_map/ppermute | solution.py:278
  144.0 11.3 %collective-permute-start.28 = (bf16[768,256]{1,0:T(8,128)(2,1)}, bf16[768,256]{1,0:T(8,128)(2,1)}, u32[]{:S(2)}, u32[]{:S(2)}) collective-permute-start(bf16[768,256]{1,0:T(8,128)(2,1)} %get-tuple-element.38), channel_id=1, source_target_pairs={{0,1},{4,5},{8,9},{12,13},{16,17},{20,21},{24,25},{28,29}} | collective-permute-start | bytes 1179656 | tf_op jit(solution)/shard_map/ppermute | solution.py:273
  146.1 10.0 %collective-permute-start.30 = (bf16[768,256]{1,0:T(8,128)(2,1)}, bf16[768,256]{1,0:T(8,128)(2,1)}, u32[]{:S(2)}, u32[]{:S(2)}) collective-permute-start(bf16[768,256]{1,0:T(8,128)(2,1)} %get-tuple-element.39), channel_id=1, source_target_pairs={{3,2},{7,6},{11,10},{15,14},{19,18},{23,22},{27,26},{31,30}} | collective-permute-start | bytes 1179656 | tf_op jit(solution)/shard_map/ppermute | solution.py:278
  149.7 11.4 %collective-permute-start.18 = (bf16[768,256]{1,0:T(8,128)(2,1)}, bf16[768,256]{1,0:T(8,128)(2,1)}, u32[]{:S(2)}, u32[]{:S(2)}) collective-permute-start(bf16[768,256]{1,0:T(8,128)(2,1)} %get-tuple-element.69), channel_id=1, source_target_pairs={{0,1},{1,2},{4,5},{5,6},{8,9},{9,10},{12,13},{13,14},{16,17},{17,1... | collective-permute-start | bytes 1179656 | tf_op jit(solution)/shard_map/ppermute | solution.py:273
  152.5 9.9 %collective-permute-start.20 = (bf16[768,256]{1,0:T(8,128)(2,1)}, bf16[768,256]{1,0:T(8,128)(2,1)}, u32[]{:S(2)}, u32[]{:S(2)}) collective-permute-start(bf16[768,256]{1,0:T(8,128)(2,1)} %get-tuple-element.68), channel_id=1, source_target_pairs={{3,2},{2,1},{7,6},{6,5},{11,10},{10,9},{15,14},{14,13},{19,18},{18... | collective-permute-start | bytes 1179656 | tf_op jit(solution)/shard_map/ppermute | solution.py:278
  154.7 17.5 %collective-permute-start.32 = (bf16[1,2,2,384,128]{4,3,2,1,0:T(8,128)(2,1)S(1)}, bf16[1,2,2,384,128]{4,3,2,1,0:T(8,128)(2,1)S(1)}, u32[]{:S(2)}, u32[]{:S(2)}) collective-permute-start(bf16[1,2,2,384,128]{4,3,2,1,0:T(8,128)(2,1)S(1)} %get-tuple-element.40.refs_11_), channel_id=1, source_target_pairs={{1,2},{2,3},{5,6},{6,7},{9,10},{10,11},{13,14},{14,15},{17,18},{18... | collective-permute-start | bytes 1179656 | tf_op jit(solution)/shard_map/ppermute | solution.py:273
  155.4 19.0 %collective-permute-start.37 = (bf16[1,2,2,384,128]{4,3,2,1,0:T(8,128)(2,1)}, bf16[1,2,2,384,128]{4,3,2,1,0:T(8,128)(2,1)S(1)}, u32[]{:S(2)}, u32[]{:S(2)}) collective-permute-start(bf16[1,2,2,384,128]{4,3,2,1,0:T(8,128)(2,1)} %copy-done.2), channel_id=1, source_target_pairs={{2,3},{6,7},{10,11},{14,15},{18,19},{22,23},{26,27},{30,31}} | collective-permute-start | bytes 1179656 | tf_op jit(solution)/shard_map/ppermute | solution.py:273
  156.1 22.1 %collective-permute-start.39 = (bf16[1,2,2,384,128]{4,3,2,1,0:T(8,128)(2,1)}, bf16[1,2,2,384,128]{4,3,2,1,0:T(8,128)(2,1)S(1)}, u32[]{:S(2)}, u32[]{:S(2)}) collective-permute-start(bf16[1,2,2,384,128]{4,3,2,1,0:T(8,128)(2,1)} %collective-permute-done.38.refs_15_), channel_id=1, source_target_pairs={{1,0},{5,4},{9,8},{13,12},{17,16},{21,20},{25,24},{29,28}} | collective-permute-start | bytes 1179656 | tf_op jit(solution)/shard_map/ppermute | solution.py:278
  161.1 33.2 %collective-permute-start.34 = (bf16[1,2,2,384,128]{4,3,2,1,0:T(8,128)(2,1)S(1)}, bf16[1,2,2,384,128]{4,3,2,1,0:T(8,128)(2,1)S(1)}, u32[]{:S(2)}, u32[]{:S(2)}) collective-permute-start(bf16[1,2,2,384,128]{4,3,2,1,0:T(8,128)(2,1)S(1)} %get-tuple-element.73.refs_14_), channel_id=1, source_target_pairs={{2,1},{1,0},{6,5},{5,4},{10,9},{9,8},{14,13},{13,12},{18,17},{17,1... | collective-permute-start | bytes 1179656 | tf_op jit(solution)/shard_map/ppermute | solution.py:278
  162.4 38.0 %collective-permute-start.29 = (bf16[768,256]{1,0:T(8,128)(2,1)}, bf16[768,256]{1,0:T(8,128)(2,1)}, u32[]{:S(2)}, u32[]{:S(2)}) collective-permute-start(bf16[768,256]{1,0:T(8,128)(2,1)} %get-tuple-element.65), channel_id=1, source_target_pairs={{0,1},{1,2},{4,5},{5,6},{8,9},{9,10},{12,13},{13,14},{16,17},{17,1... | collective-permute-start | bytes 1179656 | tf_op jit(solution)/shard_map/ppermute | solution.py:273
  173.0 28.2 %collective-permute-start.31 = (bf16[768,256]{1,0:T(8,128)(2,1)}, bf16[768,256]{1,0:T(8,128)(2,1)}, u32[]{:S(2)}, u32[]{:S(2)}) collective-permute-start(bf16[768,256]{1,0:T(8,128)(2,1)} %get-tuple-element.64), channel_id=1, source_target_pairs={{3,2},{2,1},{7,6},{6,5},{11,10},{10,9},{15,14},{14,13},{19,18},{18... | collective-permute-start | bytes 1179656 | tf_op jit(solution)/shard_map/ppermute | solution.py:278
  174.4 28.0 %collective-permute-start.21 = (bf16[768,256]{1,0:T(8,128)(2,1)}, bf16[768,256]{1,0:T(8,128)(2,1)}, u32[]{:S(2)}, u32[]{:S(2)}) collective-permute-start(bf16[768,256]{1,0:T(8,128)(2,1)} %get-tuple-element.67), channel_id=1, source_target_pairs={{0,1},{1,2},{2,3},{4,5},{5,6},{6,7},{8,9},{9,10},{10,11},{12,13},{... | collective-permute-start | bytes 1179656 | tf_op jit(solution)/shard_map/ppermute | solution.py:273
  178.2 25.1 %collective-permute-start.22 = (bf16[768,256]{1,0:T(8,128)(2,1)}, bf16[768,256]{1,0:T(8,128)(2,1)}, u32[]{:S(2)}, u32[]{:S(2)}) collective-permute-start(bf16[768,256]{1,0:T(8,128)(2,1)} %get-tuple-element.66), channel_id=1, source_target_pairs={{3,2},{2,1},{1,0},{7,6},{6,5},{5,4},{11,10},{10,9},{9,8},{15,14},{... | collective-permute-start | bytes 1179656 | tf_op jit(solution)/shard_map/ppermute | solution.py:278
  195.1 14.9 %collective-permute-start.43 = (bf16[768,256]{1,0:T(8,128)(2,1)}, bf16[768,256]{1,0:T(8,128)(2,1)}, u32[]{:S(2)}, u32[]{:S(2)}) collective-permute-start(bf16[768,256]{1,0:T(8,128)(2,1)} %get-tuple-element.53), channel_id=1, source_target_pairs={{0,1},{4,5},{8,9},{12,13},{16,17},{20,21},{24,25},{28,29}} | collective-permute-start | bytes 1179656 | tf_op jit(solution)/shard_map/ppermute | solution.py:273
  200.4 11.9 %collective-permute-start.33 = (bf16[1,2,2,384,128]{4,3,2,1,0:T(8,128)(2,1)}, bf16[1,2,2,384,128]{4,3,2,1,0:T(8,128)(2,1)S(1)}, u32[]{:S(2)}, u32[]{:S(2)}) collective-permute-start(bf16[1,2,2,384,128]{4,3,2,1,0:T(8,128)(2,1)} %copy-done.4), channel_id=1, source_target_pairs={{2,3},{6,7},{10,11},{14,15},{18,19},{22,23},{26,27},{30,31}} | collective-permute-start | bytes 1179656 | tf_op jit(solution)/shard_map/ppermute | solution.py:273
  201.1 15.8 %collective-permute-start.35 = (bf16[1,2,2,384,128]{4,3,2,1,0:T(8,128)(2,1)}, bf16[1,2,2,384,128]{4,3,2,1,0:T(8,128)(2,1)S(1)}, u32[]{:S(2)}, u32[]{:S(2)}) collective-permute-start(bf16[1,2,2,384,128]{4,3,2,1,0:T(8,128)(2,1)} %copy-done.8), channel_id=1, source_target_pairs={{1,0},{5,4},{9,8},{13,12},{17,16},{21,20},{25,24},{29,28}} | collective-permute-start | bytes 1179656 | tf_op jit(solution)/shard_map/ppermute | solution.py:278
  202.5 37.9 %collective-permute-start.46 = (bf16[768,256]{1,0:T(8,128)(2,1)}, bf16[768,256]{1,0:T(8,128)(2,1)S(1)}, u32[]{:S(2)}, u32[]{:S(2)}) collective-permute-start(bf16[768,256]{1,0:T(8,128)(2,1)} %copy-done.26), channel_id=1, source_target_pairs={{3,2},{7,6},{11,10},{15,14},{19,18},{23,22},{27,26},{31,30}} | collective-permute-start | bytes 1179656 | tf_op jit(solution)/shard_map/ppermute | solution.py:278
  205.2 39.9 %collective-permute-start.41 = (bf16[768,256]{1,0:T(8,128)(2,1)S(1)}, bf16[768,256]{1,0:T(8,128)(2,1)S(1)}, u32[]{:S(2)}, u32[]{:S(2)}) collective-permute-start(bf16[768,256]{1,0:T(8,128)(2,1)S(1)} %get-tuple-element.58), channel_id=1, source_target_pairs={{0,1},{1,2},{2,3},{4,5},{5,6},{6,7},{8,9},{9,10},{10,11},{12,13},{... | collective-permute-start | bytes 1179656 | tf_op jit(solution)/shard_map/ppermute | solution.py:273
  209.9 35.4 %collective-permute-start.42 = (bf16[768,256]{1,0:T(8,128)(2,1)S(1)}, bf16[768,256]{1,0:T(8,128)(2,1)S(1)}, u32[]{:S(2)}, u32[]{:S(2)}) collective-permute-start(bf16[768,256]{1,0:T(8,128)(2,1)S(1)} %get-tuple-element.59), channel_id=1, source_target_pairs={{3,2},{2,1},{1,0},{7,6},{6,5},{5,4},{11,10},{10,9},{9,8},{15,14},{... | collective-permute-start | bytes 1179656 | tf_op jit(solution)/shard_map/ppermute | solution.py:278
  212.3 28.1 %collective-permute-start.44 = (bf16[768,256]{1,0:T(8,128)(2,1)S(1)}, bf16[768,256]{1,0:T(8,128)(2,1)S(1)}, u32[]{:S(2)}, u32[]{:S(2)}) collective-permute-start(bf16[768,256]{1,0:T(8,128)(2,1)S(1)} %fusion.7), channel_id=1, source_target_pairs={{0,1},{1,2},{4,5},{5,6},{8,9},{9,10},{12,13},{13,14},{16,17},{17,1... | collective-permute-start | bytes 1179656 | tf_op jit(solution)/shard_map/ppermute | solution.py:273
  230.9 8.6 %collective-permute-start.49 = (bf16[768,256]{1,0:T(8,128)(2,1)S(1)}, bf16[768,256]{1,0:T(8,128)(2,1)S(1)}, u32[]{:S(2)}, u32[]{:S(2)}) collective-permute-start(bf16[768,256]{1,0:T(8,128)(2,1)S(1)} %get-tuple-element.56), channel_id=1, source_target_pairs={{0,1},{4,5},{8,9},{12,13},{16,17},{20,21},{24,25},{28,29}} | collective-permute-start | bytes 1179656 | tf_op jit(solution)/shard_map/ppermute | solution.py:273
  239.5 7.7 %collective-permute-start.52 = (bf16[768,256]{1,0:T(8,128)(2,1)S(1)}, bf16[768,256]{1,0:T(8,128)(2,1)S(1)}, u32[]{:S(2)}, u32[]{:S(2)}) collective-permute-start(bf16[768,256]{1,0:T(8,128)(2,1)S(1)} %get-tuple-element.57), channel_id=1, source_target_pairs={{3,2},{7,6},{11,10},{15,14},{19,18},{23,22},{27,26},{31,30}} | collective-permute-start | bytes 1179656 | tf_op jit(solution)/shard_map/ppermute | solution.py:278
  240.3 56.4 %collective-permute-start.40 = (bf16[2,2,512,1024]{3,2,1,0:T(8,128)(2,1)}, bf16[2,2,512,1024]{3,2,1,0:T(8,128)(2,1)}, u32[]{:S(2)}, u32[]{:S(2)}) collective-permute-start(bf16[2,2,512,1024]{3,2,1,0:T(8,128)(2,1)} %get-tuple-element.46), channel_id=1, source_target_pairs={{0,16},{16,0},{1,17},{17,1},{2,18},{18,2},{3,19},{19,3},{4,20},{20... | collective-permute-start | bytes 12582920 | tf_op jit(solution)/shard_map/ppermute | solution.py:264
  240.4 13.8 %collective-permute-start.50 = (bf16[768,256]{1,0:T(8,128)(2,1)S(1)}, bf16[768,256]{1,0:T(8,128)(2,1)S(1)}, u32[]{:S(2)}, u32[]{:S(2)}) collective-permute-start(bf16[768,256]{1,0:T(8,128)(2,1)S(1)} %fusion.2), channel_id=1, source_target_pairs={{0,1},{1,2},{4,5},{5,6},{8,9},{9,10},{12,13},{13,14},{16,17},{17,1... | collective-permute-start | bytes 1179656 | tf_op jit(solution)/shard_map/ppermute | solution.py:273
  245.1 43.4 %collective-permute-start.55 = (f32[384,256]{1,0:T(8,128)}, f32[384,256]{1,0:T(8,128)S(1)}, u32[]{:S(2)}, u32[]{:S(2)}) collective-permute-start(f32[384,256]{1,0:T(8,128)} %get-tuple-element.79), channel_id=1, source_target_pairs={{0,16},{16,0},{1,17},{17,1},{2,18},{18,2},{3,19},{19,3},{4,20},{20... | collective-permute-start | bytes 1179656 | tf_op jit(solution)/shard_map/ppermute | solution.py:264
  245.3 9.9 %collective-permute-start.47 = (bf16[768,256]{1,0:T(8,128)(2,1)S(1)}, bf16[768,256]{1,0:T(8,128)(2,1)S(1)}, u32[]{:S(2)}, u32[]{:S(2)}) collective-permute-start(bf16[768,256]{1,0:T(8,128)(2,1)S(1)} %get-tuple-element.61), channel_id=1, source_target_pairs={{3,2},{2,1},{7,6},{6,5},{11,10},{10,9},{15,14},{14,13},{19,18},{18... | collective-permute-start | bytes 1179656 | tf_op jit(solution)/shard_map/ppermute | solution.py:278
  247.3 15.0 %collective-permute-start.45 = (bf16[768,256]{1,0:T(8,128)(2,1)S(1)}, bf16[768,256]{1,0:T(8,128)(2,1)S(1)}, u32[]{:S(2)}, u32[]{:S(2)}) collective-permute-start(bf16[768,256]{1,0:T(8,128)(2,1)S(1)} %get-tuple-element.60), channel_id=1, source_target_pairs={{0,1},{1,2},{2,3},{4,5},{5,6},{6,7},{8,9},{9,10},{10,11},{12,13},{... | collective-permute-start | bytes 1179656 | tf_op jit(solution)/shard_map/ppermute | solution.py:273
  254.5 2.9 collective-permute-start.53
  255.3 17.7 %collective-permute-start.48 = (bf16[768,256]{1,0:T(8,128)(2,1)S(1)}, bf16[768,256]{1,0:T(8,128)(2,1)S(1)}, u32[]{:S(2)}, u32[]{:S(2)}) collective-permute-start(bf16[768,256]{1,0:T(8,128)(2,1)S(1)} %fusion.6), channel_id=1, source_target_pairs={{3,2},{2,1},{1,0},{7,6},{6,5},{5,4},{11,10},{10,9},{9,8},{15,14},{... | collective-permute-start | bytes 1179656 | tf_op jit(solution)/shard_map/ppermute | solution.py:278
  257.4 31.2 %collective-permute-start.56 = (f32[384,256]{1,0:T(8,128)}, f32[384,256]{1,0:T(8,128)S(1)}, u32[]{:S(2)}, u32[]{:S(2)}) collective-permute-start(f32[384,256]{1,0:T(8,128)} %get-tuple-element.81), channel_id=1, source_target_pairs={{0,16},{16,0},{1,17},{17,1},{2,18},{18,2},{3,19},{19,3},{4,20},{20... | collective-permute-start | bytes 1179656 | tf_op jit(solution)/shard_map/ppermute | solution.py:264
  262.2 19.7 %collective-permute-start.51 = (bf16[768,256]{1,0:T(8,128)(2,1)S(1)}, bf16[768,256]{1,0:T(8,128)(2,1)S(1)}, u32[]{:S(2)}, u32[]{:S(2)}) collective-permute-start(bf16[768,256]{1,0:T(8,128)(2,1)S(1)} %get-tuple-element.62), channel_id=1, source_target_pairs={{0,1},{1,2},{2,3},{4,5},{5,6},{6,7},{8,9},{9,10},{10,11},{12,13},{... | collective-permute-start | bytes 1179656 | tf_op jit(solution)/shard_map/ppermute | solution.py:273
  273.0 14.1 %collective-permute-start.54 = (bf16[768,256]{1,0:T(8,128)(2,1)S(1)}, bf16[768,256]{1,0:T(8,128)(2,1)S(1)}, u32[]{:S(2)}, u32[]{:S(2)}) collective-permute-start(bf16[768,256]{1,0:T(8,128)(2,1)S(1)} %fusion.1), channel_id=1, source_target_pairs={{3,2},{2,1},{1,0},{7,6},{6,5},{5,4},{11,10},{10,9},{9,8},{15,14},{... | collective-permute-start | bytes 1179656 | tf_op jit(solution)/shard_map/ppermute | solution.py:278
  282.0 7.3 %collective-permute-start.57 = (f32[384,256]{1,0:T(8,128)}, f32[384,256]{1,0:T(8,128)}, u32[]{:S(2)}, u32[]{:S(2)}) collective-permute-start(f32[384,256]{1,0:T(8,128)} %get-tuple-element.83), channel_id=1, source_target_pairs={{0,16},{16,0},{1,17},{17,1},{2,18},{18,2},{3,19},{19,3},{4,20},{20... | collective-permute-start | bytes 1179656 | tf_op jit(solution)/shard_map/ppermute | solution.py:264
  288.0 2.5 collective-permute-start.58
  (28 other events, 298.5 us)
